TPU v7x, 256 devices: a whole 4x4x8 slice. The times are simulated.
256 devices in a mesh: outer: 16 (over x, y), inner: 16 (over z, core).
Axes of the slice: x: 4, y: 4, z: 8, core: 2. Of those that a mesh axis runs over, the one named last changes fastest.
Arguments:
- queries: bfloat16 [65536, 2048], P(('outer', 'inner')), may hold values from -16 to 16
- keys: bfloat16 [65536, 2048], P(('outer', 'inner')), may hold values from -4 to 4
- values: bfloat16 [65536, 2048], P(('outer', 'inner')), may hold values from -24 to 24
Outputs:
- attended: bfloat16 [65536, 2048], P(('outer', 'inner'))
All inputs are finite; a program needn't handle non-finite values.
Results may differ from a plain program's by a relative error of at most 0.023.
Values may be sent and summed in bfloat16 or wider, within the bound.
No kernel may reach another device: no remote copies, remote signals or barrier semaphores. Data moves between devices by JAX's collectives and lax.ppermute only.
A program may use at most 128 MiB of HBM per device.

v0:
```python
import math

import jax
import jax.numpy as jnp
from jax import lax
from jax.experimental import pallas as pl
from jax.experimental.pallas import tpu as pltpu
from jax.sharding import PartitionSpec as P

HEADS = 16
HD = 128
AXES = ("outer", "inner")
SCALE = math.log2(math.e) / math.sqrt(HD)
STEP_HEADS = 4
STEP_COLS = STEP_HEADS * HD
VMEM_LIMIT = 24 * 1024 * 1024


def averaging(rows, cols, row_span, col_span, weight):
    row = lax.broadcasted_iota(jnp.int32, (rows, cols), 0) // row_span
    col = lax.broadcasted_iota(jnp.int32, (rows, cols), 1) // col_span
    return jnp.where(row == col, weight, 0.0).astype(jnp.bfloat16)


def dot_f32(a, b):
    return lax.dot_general(a, b, (((1,), (0,)), ((), ())), preferred_element_type=jnp.float32)


def dot_nt(a, b):
    return lax.dot_general(a, b, (((1,), (1,)), ((), ())), preferred_element_type=jnp.float32)


def dot_bf16(a, b):
    return dot_f32(a, b).astype(jnp.bfloat16)


def summary_kernel(q_ref, k_ref, v_ref, first_ref, heads_ref, last_ref):
    rows = q_ref.shape[0]
    halves = [averaging(rows >> (i + 1), rows >> i, 1, 2, 0.5) for i in range(4)]
    levels = []
    for index, ref in enumerate((k_ref, v_ref)):
        current = ref[...]
        for matrix in halves[:2]:
            current = dot_bf16(matrix, current)
        first_ref[index] = current
        second = dot_bf16(halves[2], current)
        third = dot_bf16(halves[3], second)
        levels.append((second, third))
    coarse = dot_bf16(averaging(rows // 8, rows, 1, 8, 0.125), q_ref[...])
    n3 = rows // 16
    row = lax.broadcasted_iota(jnp.int32, (n3, n3), 0)
    col = lax.broadcasted_iota(jnp.int32, (n3, n3), 1) // 2
    place_k = jnp.where(row == col, 0.5, 0.0).astype(jnp.bfloat16)
    place_v = jnp.where(row == col + n3 // 2, 0.5, 0.0).astype(jnp.bfloat16)
    last = (dot_f32(place_k, levels[0][1]) + dot_f32(place_v, levels[1][1])).astype(jnp.bfloat16)
    n2 = rows // 8
    for h in range(STEP_HEADS):
        cols = slice(h * HD, (h + 1) * HD)
        heads_ref[h, 0:n2, :] = levels[0][0][:, cols]
        heads_ref[h, n2 : 2 * n2, :] = levels[1][0][:, cols]
        heads_ref[h, 2 * n2 : 3 * n2, :] = coarse[:, cols]
        last_ref[h] = last[:, cols]


def summaries(queries, keys, values):
    rows, width = queries.shape
    block = pl.BlockSpec((rows, STEP_COLS), lambda i: (0, i))
    return pl.pallas_call(
        summary_kernel,
        grid=(width // STEP_COLS,),
        in_specs=[block, block, block],
        out_specs=[
            pl.BlockSpec((2, rows // 4, STEP_COLS), lambda i: (0, 0, i)),
            pl.BlockSpec((STEP_HEADS, 3 * rows // 8, HD), lambda i: (i, 0, 0)),
            pl.BlockSpec((STEP_HEADS, rows // 16, HD), lambda i: (i, 0, 0)),
        ],
        out_shape=[
            jax.ShapeDtypeStruct((2, rows // 4, width), jnp.bfloat16),
            jax.ShapeDtypeStruct((HEADS, 3 * rows // 8, HD), jnp.bfloat16),
            jax.ShapeDtypeStruct((HEADS, rows // 16, HD), jnp.bfloat16),
        ],
        compiler_params=pltpu.CompilerParams(vmem_limit_bytes=VMEM_LIMIT),
        cost_estimate=pl.CostEstimate(flops=400_000_000, bytes_accessed=5_000_000, transcendentals=0),
        name="summaries",
    )(queries, keys, values)


def with_ones(value):
    return jnp.concatenate([value, jnp.ones_like(value)], 1)


def far_kernel(recv_ref, sib_ref, out_ref):
    blocks = recv_ref.shape[0]
    n2 = recv_ref.shape[1] // 3
    total = blocks * n2
    keys2 = recv_ref[:, 0:n2, :].reshape(total, HD)
    values2 = recv_ref[:, n2 : 2 * n2, :].reshape(total, HD)
    query2 = recv_ref[:, 2 * n2 : 3 * n2, :].reshape(total, HD)
    last = sib_ref[...].reshape(-1, HD)
    rows4 = last.shape[0] // 2
    row = lax.broadcasted_iota(jnp.int32, (rows4, 2 * rows4), 0)
    col = lax.broadcasted_iota(jnp.int32, (rows4, 2 * rows4), 1)
    span = sib_ref.shape[1] // 2
    spot = row + (row // span) * span
    keys4 = dot_bf16(jnp.where(col == spot, 1.0, 0.0).astype(jnp.bfloat16), last)
    values4 = dot_bf16(jnp.where(col == spot + span, 1.0, 0.0).astype(jnp.bfloat16), last)
    group = total // 4
    half = averaging(group // 2, group, 1, 2, 0.5)
    keys3 = [dot_bf16(half, keys2[i * group : (i + 1) * group]) for i in range(4)]
    values3 = [dot_bf16(half, values2[i * group : (i + 1) * group]) for i in range(4)]
    spread2 = averaging(group, group, 2, 2, 0.5)
    spread4 = averaging(group, group, 4, 4, 0.25)
    eye = (
        lax.broadcasted_iota(jnp.int32, (group, group), 0)
        == lax.broadcasted_iota(jnp.int32, (group, group), 1)
    )
    group_blocks = blocks // 4
    pad_row = lax.broadcasted_iota(jnp.int32, (16, group), 0)
    for g in range(4):
        own = query2[g * group : (g + 1) * group]
        sib = g ^ 1
        far = 2 * ((g // 2) ^ 1)
        key3 = jnp.concatenate(keys3[far : far + 2], 0)
        value3 = jnp.concatenate(values3[far : far + 2], 0)
        scores = [
            dot_nt(own, keys2[sib * group : (sib + 1) * group]) * SCALE + 3.0,
            dot_nt(dot_bf16(spread2, own), key3) * SCALE + 4.0,
            dot_nt(dot_bf16(spread4, own), keys4) * SCALE + 5.0,
        ]
        scores = jnp.concatenate(scores, 1)
        peak = jnp.max(scores, axis=1, keepdims=True)
        weights = jnp.exp2(scores - peak).astype(jnp.bfloat16)
        value = jnp.concatenate([values2[sib * group : (sib + 1) * group], value3, values4], 0)
        both = dot_f32(weights, with_ones(value))
        total_weight = both[:, HD:]
        mean = (both[:, :HD] / total_weight).astype(jnp.bfloat16)
        level = peak + jnp.log2(total_weight)
        level_row = jnp.sum(jnp.where(eye, level, 0.0), axis=0, keepdims=True)
        high = level_row.astype(jnp.bfloat16).astype(jnp.float32)
        rest = level_row - high
        mid = rest.astype(jnp.bfloat16).astype(jnp.float32)
        low = rest - mid
        packed = jnp.where(pad_row == 0, high, jnp.where(pad_row == 1, mid, low)).astype(jnp.bfloat16)
        for j in range(group_blocks):
            out_ref[g * group_blocks + j, 0:n2, :] = mean[j * n2 : (j + 1) * n2]
            out_ref[g * group_blocks + j, n2 : n2 + 16, :] = packed


def far_attention(received, sibling):
    blocks, packed_rows, _ = received.shape
    n2 = packed_rows // 3
    return pl.pallas_call(
        far_kernel,
        out_shape=jax.ShapeDtypeStruct((blocks, n2 + 16, HD), jnp.bfloat16),
        compiler_params=pltpu.CompilerParams(vmem_limit_bytes=VMEM_LIMIT),
        cost_estimate=pl.CostEstimate(
            flops=200_000_000, bytes_accessed=1_000_000, transcendentals=200_000
        ),
        name="far_attention",
    )(received, sibling)


def near_kernel(
    bias_ref, q_ref, k_ref, v_ref, kb_ref, vb_ref, ka_ref, va_ref, f1_ref, f2_ref, out_ref, level_ref
):
    rows = q_ref.shape[0]
    step = pl.program_id(0)
    coarse = dot_bf16(averaging(rows, rows, 4, 4, 0.25), q_ref[...])
    lane = lax.broadcasted_iota(jnp.int32, (rows, HD), 1)
    levels = jnp.zeros((rows, HD), jnp.float32)
    for h in range(STEP_HEADS):
        cols = slice(h * HD, (h + 1) * HD)
        query = q_ref[:, cols]
        far_key = jnp.concatenate([f1_ref[0, :, cols], f2_ref[0, :, cols]], 0)
        far_value = jnp.concatenate([f1_ref[1, :, cols], f2_ref[1, :, cols]], 0)
        scores = [
            dot_nt(query, k_ref[:, cols]) * SCALE,
            dot_nt(query, kb_ref[:, cols]) * SCALE + bias_ref[0],
            dot_nt(query, ka_ref[:, cols]) * SCALE + bias_ref[1],
            dot_nt(coarse[:, cols], far_key) * SCALE + 2.0,
        ]
        scores = jnp.concatenate(scores, 1)
        peak = jnp.max(scores, axis=1, keepdims=True)
        weights = jnp.exp2(scores - peak).astype(jnp.bfloat16)
        value = jnp.concatenate([v_ref[:, cols], vb_ref[:, cols], va_ref[:, cols], far_value], 0)
        both = dot_f32(weights, with_ones(value))
        total_weight = both[:, HD:]
        out_ref[:, cols] = (both[:, :HD] / total_weight).astype(jnp.bfloat16)
        level = peak + jnp.log2(total_weight)
        levels = jnp.where(lane == step * STEP_HEADS + h, level, levels)

    @pl.when(step == 0)
    def _():
        level_ref[...] = levels

    @pl.when(step > 0)
    def _():
        level_ref[...] = level_ref[...] + levels


def near_attention(bias, q, k, v, k_before, v_before, k_after, v_after, far1, far2):
    rows, width = q.shape
    block = pl.BlockSpec((rows, STEP_COLS), lambda i: (0, i))
    far_block = pl.BlockSpec((2, rows // 4, STEP_COLS), lambda i: (0, 0, i))
    return pl.pallas_call(
        near_kernel,
        grid=(width // STEP_COLS,),
        in_specs=[pl.BlockSpec(memory_space=pltpu.SMEM)] + [block] * 7 + [far_block] * 2,
        out_specs=[block, pl.BlockSpec((rows, HD), lambda i: (0, 0))],
        out_shape=[
            jax.ShapeDtypeStruct((rows, width), jnp.bfloat16),
            jax.ShapeDtypeStruct((rows, HD), jnp.float32),
        ],
        compiler_params=pltpu.CompilerParams(vmem_limit_bytes=VMEM_LIMIT),
        cost_estimate=pl.CostEstimate(
            flops=4_000_000_000, bytes_accessed=10_000_000, transcendentals=4_000_000
        ),
        name="near_attention",
    )(bias, q, k, v, k_before, v_before, k_after, v_after, far1, far2)


def combine_kernel(spot_ref, near_ref, level_ref, far_ref, out_ref):
    rows = near_ref.shape[0]
    n2 = far_ref.shape[1] - 16
    factor = rows // n2
    row = lax.broadcasted_iota(jnp.int32, (rows, HD), 0) // factor
    lane = lax.broadcasted_iota(jnp.int32, (rows, HD), 1)
    pick = jnp.where(lane == row + spot_ref[0], 1.0, 0.0).astype(jnp.bfloat16)
    spread = averaging(rows, n2, factor, 1, 1.0)
    parts = far_ref[:, n2 : n2 + 16, :]
    packed = parts.reshape(HEADS * 16, HD)
    spread_levels = dot_nt(pick, packed)
    heads = lax.broadcasted_iota(jnp.int32, (rows, HD), 1)
    for h in range(HEADS):
        cols = slice(h * HD, (h + 1) * HD)
        far_level = (
            spread_levels[:, 16 * h : 16 * h + 1]
            + spread_levels[:, 16 * h + 1 : 16 * h + 2]
            + spread_levels[:, 16 * h + 2 : 16 * h + 3]
        )
        near_part = 1.0 / (1.0 + jnp.exp2(far_level - level_ref[:, h : h + 1]))
        far_mean = dot_f32(spread, far_ref[h, 0:n2, :])
        near_mean = near_ref[:, cols].astype(jnp.float32)
        out_ref[:, cols] = (far_mean + near_part * (near_mean - far_mean)).astype(jnp.bfloat16)


def combine(spot, near_mean, near_level, far):
    return pl.pallas_call(
        combine_kernel,
        in_specs=[pl.BlockSpec(memory_space=pltpu.SMEM)]
        + [pl.BlockSpec(memory_space=pltpu.VMEM)] * 3,
        out_specs=pl.BlockSpec(memory_space=pltpu.VMEM),
        out_shape=jax.ShapeDtypeStruct(near_mean.shape, jnp.bfloat16),
        compiler_params=pltpu.CompilerParams(vmem_limit_bytes=VMEM_LIMIT),
        name="combine",
    )(spot, near_mean, near_level, far)


def body(queries, keys, values):
    devices = lax.axis_size(AXES)
    inner = lax.axis_size("inner")
    index = lax.axis_index(AXES)
    rows = queries.shape[0]
    n2 = rows // 8

    def exchange(value, stride):
        return lax.ppermute(value, AXES, [(i, i ^ stride) for i in range(devices)])

    first, heads, last = summaries(queries, keys, values)
    sibling = exchange(last, inner)
    up = [(i, i + 1) for i in range(devices - 1)]
    down = [(i + 1, i) for i in range(devices - 1)]
    packed = jnp.concatenate([heads, sibling], 1)
    received = lax.all_to_all(packed, "inner", 0, 0, tiled=True)
    far1 = exchange(first, 2)
    far2 = exchange(far1, 1)
    k_before = lax.ppermute(keys, AXES, up)
    k_after = lax.ppermute(keys, AXES, down)
    v_before = lax.ppermute(values, AXES, up)
    v_after = lax.ppermute(values, AXES, down)
    far = far_attention(received[:, : 3 * n2], received[:, 3 * n2 :])
    far = lax.all_to_all(far, "inner", 0, 0, tiled=True)
    lowest = jnp.float32(-1e30)
    bias = jnp.stack(
        [jnp.where(index == 0, lowest, 0.0), jnp.where(index == devices - 1, lowest, 0.0)]
    )
    near_mean, near_level = near_attention(
        bias, queries, keys, values, k_before, v_before, k_after, v_after, far1, far2
    )
    spot = (index % (inner // 4) * n2).reshape(1).astype(jnp.int32)
    return combine(spot, near_mean, near_level, far)


def solution(mesh):
    spec = P(AXES, None)
    return jax.shard_map(
        body, mesh=mesh, in_specs=(spec, spec, spec), out_specs=spec, check_vma=False
    )
```

profile of v0, /device:TPU:1, one launch (start us, length us, event | category | flops | bytes accessed | tf_op | source)
XLA Modules:
  0.0 83.1 jit_solution(10979971177085041864)
XLA Ops:
  0.0 0.0 copy-start
  0.0 1.2 %copy-done = bf16[256,2048]{1,0:T(8,128)(2,1)S(1)} copy-done((bf16[256,2048]{1,0:T(8,128)(2,1)S(1)}, bf16[256,2048]{1,0:T(8,128)(2,1)}, u32[]{:S(2)}) %copy-start) | copy-done | bytes 1048600
  1.2 5.6 %summaries.1 = (bf16[2,64,2048]{2,1,0:T(8,128)(2,1)S(1)}, bf16[16,96,128]{2,1,0:T(8,128)(2,1)S(1)}, bf16[16,16,128]{2,1,0:T(8,128)(2,1)S(1)}) custom-call(bf16[256,2048]{1,0:T(8,128)(2,1)S(1)} %copy-done, bf16[256,2048]{1,0:T(8,128)(2,1)} %k_ref.3, bf16[256,2048]{1,0:T(8,128)(2,1)} %v_ref.3), custom_call_target="tpu_custom_call" | custom-call | flops 400000000 | bytes 5000000 | tf_op jit(solution)/shard_map/summaries/pallas_call | solution.py:68
  6.9 2.2 %collective-permute-start.6 = (bf16[16,16,128]{2,1,0:T(8,128)(2,1)S(1)}, bf16[16,16,128]{2,1,0:T(8,128)(2,1)S(1)}, u32[]{:S(2)}, u32[]{:S(2)}) collective-permute-start(bf16[16,16,128]{2,1,0:T(8,128)(2,1)S(1)} %get-tuple-element.14), channel_id=1, source_target_pairs={{0,16},{1,17},{2,18},{3,19},{4,20},{5,21},{6,22},{7,23},{8,24},{9,... | collective-permute-start | bytes 196616 | tf_op jit(solution)/shard_map/ppermute | solution.py:267
  9.0 1.6 %collective-permute-start.4 = (bf16[2,64,2048]{2,1,0:T(8,128)(2,1)S(1)}, bf16[2,64,2048]{2,1,0:T(8,128)(2,1)}, u32[]{:S(2)}, u32[]{:S(2)}) collective-permute-start(bf16[2,64,2048]{2,1,0:T(8,128)(2,1)S(1)} %get-tuple-element.10), channel_id=1, source_target_pairs={{0,2},{1,3},{2,0},{3,1},{4,6},{5,7},{6,4},{7,5},{8,10},{9,11},{10,... | collective-permute-start | bytes 1572872 | tf_op jit(solution)/shard_map/ppermute | solution.py:267
  10.7 3.1 %collective-permute-start.2 = (bf16[256,2048]{1,0:T(8,128)(2,1)}, bf16[256,2048]{1,0:T(8,128)(2,1)S(1)}, u32[]{:S(2)}, u32[]{:S(2)}) collective-permute-start(bf16[256,2048]{1,0:T(8,128)(2,1)} %k_ref.3), channel_id=1, source_target_pairs={{1,0},{2,1},{3,2},{4,3},{5,4},{6,5},{7,6},{8,7},{9,8},{10,9},{11,1... | collective-permute-start | bytes 3145736 | tf_op jit(solution)/shard_map/ppermute | solution.py:278
  13.8 2.4 %collective-permute-start = (bf16[256,2048]{1,0:T(8,128)(2,1)}, bf16[256,2048]{1,0:T(8,128)(2,1)S(1)}, u32[]{:S(2)}, u32[]{:S(2)}) collective-permute-start(bf16[256,2048]{1,0:T(8,128)(2,1)} %k_ref.3), channel_id=1, source_target_pairs={{0,1},{1,2},{2,3},{3,4},{4,5},{5,6},{6,7},{7,8},{8,9},{9,10},{10,1... | collective-permute-start | bytes 3145736 | tf_op jit(solution)/shard_map/ppermute | solution.py:277
  16.2 2.0 %collective-permute-start.3 = (bf16[256,2048]{1,0:T(8,128)(2,1)}, bf16[256,2048]{1,0:T(8,128)(2,1)}, u32[]{:S(2)}, u32[]{:S(2)}) collective-permute-start(bf16[256,2048]{1,0:T(8,128)(2,1)} %v_ref.3), channel_id=1, source_target_pairs={{1,0},{2,1},{3,2},{4,3},{5,4},{6,5},{7,6},{8,7},{9,8},{10,9},{11,1... | collective-permute-start | bytes 3145736 | tf_op jit(solution)/shard_map/ppermute | solution.py:280
  18.2 0.0 collective-permute-done.6
  18.2 3.6 %collective-permute-start.1 = (bf16[256,2048]{1,0:T(8,128)(2,1)}, bf16[256,2048]{1,0:T(8,128)(2,1)}, u32[]{:S(2)}, u32[]{:S(2)}) collective-permute-start(bf16[256,2048]{1,0:T(8,128)(2,1)} %v_ref.3), channel_id=1, source_target_pairs={{0,1},{1,2},{2,3},{3,4},{4,5},{5,6},{6,7},{7,8},{8,9},{9,10},{10,1... | collective-permute-start | bytes 3145736 | tf_op jit(solution)/shard_map/ppermute | solution.py:279
  21.8 0.8 pad_maximum_fusion
  22.6 10.6 %all-to-all-start = ((bf16[16,112,128]{2,1,0:T(8,128)(2,1)}), bf16[16,112,128]{2,1,0:T(8,128)(2,1)}, u32[]{:S(2)}, u32[]{:S(2)}) async-start(bf16[16,112,128]{2,1,0:T(8,128)(2,1)} %pad_maximum_fusion), calls=%async_computation | async-start | bytes 917504 | tf_op jit(solution)/shard_map/all_to_all | solution.py:274
  33.2 0.0 collective-permute-done.4.f1_ref
  33.2 0.2 collective-permute-start.5
  33.4 0.0 copy-start.1
  33.4 0.1 pad_maximum_fusion.1.bias_ref
  33.5 25.1 %all-to-all-done = bf16[16,112,128]{2,1,0:T(8,128)(2,1)} async-done(((bf16[16,112,128]{2,1,0:T(8,128)(2,1)}), bf16[16,112,128]{2,1,0:T(8,128)(2,1)}, u32[]{:S(2)}, u32[]{:S(2)}) %all-to-all-start) | async-done | bytes 458784 | tf_op jit(solution)/shard_map/all_to_all | solution.py:274
  58.6 0.8 %slice.9.sib_ref = bf16[16,16,128]{2,1,0:T(8,128)(2,1)S(1)} slice(bf16[16,112,128]{2,1,0:T(8,128)(2,1)} %all-to-all-done), slice={[0:16], [96:112], [0:128]} | slice | bytes 131072 | tf_op jit(solution)/shard_map/slice | solution.py:281
  59.4 1.0 %slice.8.recv_ref = bf16[16,96,128]{2,1,0:T(8,128)(2,1)S(1)} slice(bf16[16,112,128]{2,1,0:T(8,128)(2,1)} %all-to-all-done), slice={[0:16], [0:96], [0:128]} | slice | bytes 786432 | tf_op jit(solution)/shard_map/slice | solution.py:281
  60.5 2.4 %far_attention.1 = bf16[16,48,128]{2,1,0:T(8,128)(2,1)} custom-call(bf16[16,96,128]{2,1,0:T(8,128)(2,1)S(1)} %slice.8.recv_ref, bf16[16,16,128]{2,1,0:T(8,128)(2,1)S(1)} %slice.9.sib_ref), custom_call_target="tpu_custom_call" | custom-call | flops 200000000 | bytes 1000000 | tf_op jit(solution)/shard_map/far_attention/pallas_call | solution.py:152
  62.8 5.8 %all-to-all-start.1 = ((bf16[16,48,128]{2,1,0:T(8,128)(2,1)}), bf16[16,48,128]{2,1,0:T(8,128)(2,1)S(1)}, u32[]{:S(2)}, u32[]{:S(2)}) async-start(bf16[16,48,128]{2,1,0:T(8,128)(2,1)} %far_attention.1), calls=%async_computation.1 | async-start | bytes 393216 | tf_op jit(solution)/shard_map/all_to_all | solution.py:282
  68.6 0.0 collective-permute-done.5.f2_ref
  68.6 0.0 collective-permute-done.2.ka_ref
  68.6 0.0 collective-permute-done.kb_ref
  68.6 0.0 copy-start.2
  68.7 1.0 %copy-done.2 = bf16[256,2048]{1,0:T(8,128)(2,1)} copy-done((bf16[256,2048]{1,0:T(8,128)(2,1)}, bf16[256,2048]{1,0:T(8,128)(2,1)S(1)}, u32[]{:S(2)}) %copy-start.2) | copy-done | bytes 1048600
  69.6 0.0 collective-permute-done.3.va_ref
  69.6 0.0 collective-permute-done.1.vb_ref
  69.6 0.0 copy-done.1
  69.6 0.0 copy-start.3
  69.6 1.2 %copy-done.3 = bf16[256,2048]{1,0:T(8,128)(2,1)S(1)} copy-done((bf16[256,2048]{1,0:T(8,128)(2,1)S(1)}, bf16[256,2048]{1,0:T(8,128)(2,1)}, u32[]{:S(2)}) %copy-start.3) | copy-done | bytes 1048600
  70.9 9.1 %near_attention.1 = (bf16[256,2048]{1,0:T(8,128)(2,1)S(1)}, f32[256,128]{1,0:T(8,128)S(1)}) custom-call(f32[2]{0:T(128)S(1)} %pad_maximum_fusion.1.bias_ref, bf16[256,2048]{1,0:T(8,128)(2,1)S(1)} %copy-done.1, bf16[256,2048]{1,0:T(8,128)(2,1)} %k_ref.3, bf16[256,2048]{1,0:T(8,128)(2,1)} %v_ref.3, bf16[256,2048]{1,0:T(8,128)(2,1)S(1)} %copy-done.3, ...), custom_call_target="tpu_custom_call" | custom-call | flops 4000000000 | bytes 10000000 | tf_op jit(solution)/shard_map/near_attention/pallas_call | solution.py:205
  79.9 0.0 all-to-all-done.1.far_ref
  79.9 3.2 %combine.1 = bf16[256,2048]{1,0:T(8,128)(2,1)} custom-call(s32[1]{0:T(128)} %bitcast.spot_ref, bf16[256,2048]{1,0:T(8,128)(2,1)S(1)} %get-tuple-element.11.near_ref, f32[256,128]{1,0:T(8,128)S(1)} %get-tuple-element.12.level_ref, bf16[16,48,128]{2,1,0:T(8,128)(2,1)S(1)} %all-to-all-done.1.far_ref), custom_call_target="tpu_custom_call" | custom-call | tf_op jit(solution)/shard_map/combine/pallas_call | solution.py:248
Async XLA Ops:
  0.0 1.2 %copy-start = (bf16[256,2048]{1,0:T(8,128)(2,1)S(1)}, bf16[256,2048]{1,0:T(8,128)(2,1)}, u32[]{:S(2)}) copy-start(bf16[256,2048]{1,0:T(8,128)(2,1)} %q_ref.3) | copy-start | bytes 3145732
  6.9 11.4 %collective-permute-start.6 = (bf16[16,16,128]{2,1,0:T(8,128)(2,1)S(1)}, bf16[16,16,128]{2,1,0:T(8,128)(2,1)S(1)}, u32[]{:S(2)}, u32[]{:S(2)}) collective-permute-start(bf16[16,16,128]{2,1,0:T(8,128)(2,1)S(1)} %get-tuple-element.14), channel_id=1, source_target_pairs={{0,16},{1,17},{2,18},{3,19},{4,20},{5,21},{6,22},{7,23},{8,24},{9,... | collective-permute-start | bytes 196616 | tf_op jit(solution)/shard_map/ppermute | solution.py:267
  9.0 24.2 %collective-permute-start.4 = (bf16[2,64,2048]{2,1,0:T(8,128)(2,1)S(1)}, bf16[2,64,2048]{2,1,0:T(8,128)(2,1)}, u32[]{:S(2)}, u32[]{:S(2)}) collective-permute-start(bf16[2,64,2048]{2,1,0:T(8,128)(2,1)S(1)} %get-tuple-element.10), channel_id=1, source_target_pairs={{0,2},{1,3},{2,0},{3,1},{4,6},{5,7},{6,4},{7,5},{8,10},{9,11},{10,... | collective-permute-start | bytes 1572872 | tf_op jit(solution)/shard_map/ppermute | solution.py:267
  10.7 58.0 %collective-permute-start.2 = (bf16[256,2048]{1,0:T(8,128)(2,1)}, bf16[256,2048]{1,0:T(8,128)(2,1)S(1)}, u32[]{:S(2)}, u32[]{:S(2)}) collective-permute-start(bf16[256,2048]{1,0:T(8,128)(2,1)} %k_ref.3), channel_id=1, source_target_pairs={{1,0},{2,1},{3,2},{4,3},{5,4},{6,5},{7,6},{8,7},{9,8},{10,9},{11,1... | collective-permute-start | bytes 3145736 | tf_op jit(solution)/shard_map/ppermute | solution.py:278
  13.8 54.8 %collective-permute-start = (bf16[256,2048]{1,0:T(8,128)(2,1)}, bf16[256,2048]{1,0:T(8,128)(2,1)S(1)}, u32[]{:S(2)}, u32[]{:S(2)}) collective-permute-start(bf16[256,2048]{1,0:T(8,128)(2,1)} %k_ref.3), channel_id=1, source_target_pairs={{0,1},{1,2},{2,3},{3,4},{4,5},{5,6},{6,7},{7,8},{8,9},{9,10},{10,1... | collective-permute-start | bytes 3145736 | tf_op jit(solution)/shard_map/ppermute | solution.py:277
  16.2 53.4 %collective-permute-start.3 = (bf16[256,2048]{1,0:T(8,128)(2,1)}, bf16[256,2048]{1,0:T(8,128)(2,1)}, u32[]{:S(2)}, u32[]{:S(2)}) collective-permute-start(bf16[256,2048]{1,0:T(8,128)(2,1)} %v_ref.3), channel_id=1, source_target_pairs={{1,0},{2,1},{3,2},{4,3},{5,4},{6,5},{7,6},{8,7},{9,8},{10,9},{11,1... | collective-permute-start | bytes 3145736 | tf_op jit(solution)/shard_map/ppermute | solution.py:280
  18.2 51.4 %collective-permute-start.1 = (bf16[256,2048]{1,0:T(8,128)(2,1)}, bf16[256,2048]{1,0:T(8,128)(2,1)}, u32[]{:S(2)}, u32[]{:S(2)}) collective-permute-start(bf16[256,2048]{1,0:T(8,128)(2,1)} %v_ref.3), channel_id=1, source_target_pairs={{0,1},{1,2},{2,3},{3,4},{4,5},{5,6},{6,7},{7,8},{8,9},{9,10},{10,1... | collective-permute-start | bytes 3145736 | tf_op jit(solution)/shard_map/ppermute | solution.py:279
  22.6 36.0 %all-to-all-start = ((bf16[16,112,128]{2,1,0:T(8,128)(2,1)}), bf16[16,112,128]{2,1,0:T(8,128)(2,1)}, u32[]{:S(2)}, u32[]{:S(2)}) async-start(bf16[16,112,128]{2,1,0:T(8,128)(2,1)} %pad_maximum_fusion), calls=%async_computation | async-start | bytes 917504 | tf_op jit(solution)/shard_map/all_to_all | solution.py:274
  33.2 35.4 %collective-permute-start.5 = (bf16[2,64,2048]{2,1,0:T(8,128)(2,1)}, bf16[2,64,2048]{2,1,0:T(8,128)(2,1)}, u32[]{:S(2)}, u32[]{:S(2)}) collective-permute-start(bf16[2,64,2048]{2,1,0:T(8,128)(2,1)} %collective-permute-done.4.f1_ref), channel_id=1, source_target_pairs={{0,1},{1,0},{2,3},{3,2},{4,5},{5,4},{6,7},{7,6},{8,9},{9,8},{10,11... | collective-permute-start | bytes 1572872 | tf_op jit(solution)/shard_map/ppermute | solution.py:267
  33.4 36.2 %copy-start.1 = (bf16[256,2048]{1,0:T(8,128)(2,1)S(1)}, bf16[256,2048]{1,0:T(8,128)(2,1)}, u32[]{:S(2)}) copy-start(bf16[256,2048]{1,0:T(8,128)(2,1)} %q_ref.3) | copy-start | bytes 3145732
  62.8 17.1 %all-to-all-start.1 = ((bf16[16,48,128]{2,1,0:T(8,128)(2,1)}), bf16[16,48,128]{2,1,0:T(8,128)(2,1)S(1)}, u32[]{:S(2)}, u32[]{:S(2)}) async-start(bf16[16,48,128]{2,1,0:T(8,128)(2,1)} %far_attention.1), calls=%async_computation.1 | async-start | bytes 393216 | tf_op jit(solution)/shard_map/all_to_all | solution.py:282
  68.6 1.0 %copy-start.2 = (bf16[256,2048]{1,0:T(8,128)(2,1)}, bf16[256,2048]{1,0:T(8,128)(2,1)S(1)}, u32[]{:S(2)}) copy-start(bf16[256,2048]{1,0:T(8,128)(2,1)S(1)} %collective-permute-done.kb_ref) | copy-start | bytes 3145732
  69.6 1.2 %copy-start.3 = (bf16[256,2048]{1,0:T(8,128)(2,1)S(1)}, bf16[256,2048]{1,0:T(8,128)(2,1)}, u32[]{:S(2)}) copy-start(bf16[256,2048]{1,0:T(8,128)(2,1)} %copy-done.2) | copy-start | bytes 3145732
where the time goes:
time: 83.7 us; the launch traced here: 83.1 us
  starting transfers between devices  31.5 us (38%)
  waiting for transfers between devices  25.1 us (30%)
  Pallas kernels  20.2 us (24%)
  local copies, waits for them, and re-layouts  5.28 us (6%)
  other arithmetic  0.87 us (1%)
    all_to_all x1, waiting for transfers between devices, body(): received = lax.all_to_all(packed, 'inner', 0, 0, tiled=True)  25.1 us
    all_to_all x1, starting transfers between devices, body(): received = lax.all_to_all(packed, 'inner', 0, 0, tiled=True)  10.6 us
    pallas_call x1, Pallas kernels, near_attention(): pl.pallas_call(near_kernel, grid=(width // STEP_COLS,), in_specs=[pl.Bloc...  9.06 us
    all_to_all x1, starting transfers between devices, body(): far = lax.all_to_all(far, 'inner', 0, 0, tiled=True)  5.78 us
    pallas_call x1, Pallas kernels, summaries(): pl.pallas_call(summary_kernel, grid=(width // STEP_COLS,), in_specs=[bloc...  5.63 us
    ppermute x3, starting transfers between devices, exchange(): return lax.ppermute(value, AXES, [(i, i ^ stride) for i in range(devices)])  4.05 us
    ppermute x1, starting transfers between devices, body(): v_before = lax.ppermute(values, AXES, up)  3.6 us
    unnamed x8, local copies, waits for them, and re-layouts  3.41 us
  transfers between devices with their start and end apart: 9, of which 1 were waited for; matrix products, arithmetic and copies ran while one was open for 3% of the time, Pallas kernels for 14%

commit v1 on v0

v1 whole, which is shorter than its diff:
```python
import functools
import math

import jax
import jax.numpy as jnp
from jax import lax
from jax.experimental import pallas as pl
from jax.experimental.pallas import tpu as pltpu
from jax.sharding import PartitionSpec as P

HEADS = 16
HD = 128
AXES = ("outer", "inner")
SCALE = math.log2(math.e) / math.sqrt(HD)
STEP_HEADS = 4
STEP_COLS = STEP_HEADS * HD
VMEM_LIMIT = 60 * 1024 * 1024


def grid_of(shape, axis, span=1):
    return lax.shift_right_logical(
        lax.broadcasted_iota(jnp.int32, shape, axis), jnp.int32(span.bit_length() - 1)
    )


def averaging(rows, cols, row_span, col_span, weight):
    same = grid_of((rows, cols), 0, row_span) == grid_of((rows, cols), 1, col_span)
    return jnp.where(same, weight, 0.0).astype(jnp.bfloat16)


def dot_f32(a, b):
    return lax.dot_general(a, b, (((1,), (0,)), ((), ())), preferred_element_type=jnp.float32)


def dot_nt(a, b):
    return lax.dot_general(a, b, (((1,), (1,)), ((), ())), preferred_element_type=jnp.float32)


def dot_bf16(a, b):
    return dot_f32(a, b).astype(jnp.bfloat16)


def summary_kernel(q_ref, k_ref, v_ref, first_ref, heads_ref, last_ref):
    rows = q_ref.shape[0]
    n1, n2, n4 = rows // 4, rows // 8, rows // 32
    nothing = jnp.zeros((n4, rows), jnp.bfloat16)
    top = [averaging(n1, rows, 1, 4, 1 / 4), averaging(n2, rows, 1, 8, 1 / 8)]
    bottom = averaging(n4, rows, 1, 32, 1 / 32)
    of_k = dot_f32(jnp.concatenate(top + [bottom, nothing], 0), k_ref[...])
    of_v = dot_f32(jnp.concatenate(top + [nothing, bottom], 0), v_ref[...])
    coarse = dot_bf16(top[1], q_ref[...])
    first_ref[0] = of_k[:n1].astype(jnp.bfloat16)
    first_ref[1] = of_v[:n1].astype(jnp.bfloat16)
    second_k = of_k[n1 : n1 + n2].astype(jnp.bfloat16)
    second_v = of_v[n1 : n1 + n2].astype(jnp.bfloat16)
    last = (of_k[n1 + n2 :] + of_v[n1 + n2 :]).astype(jnp.bfloat16)
    for h in range(STEP_HEADS):
        cols = slice(h * HD, (h + 1) * HD)
        heads_ref[h, 0:n2, :] = second_k[:, cols]
        heads_ref[h, n2 : 2 * n2, :] = second_v[:, cols]
        heads_ref[h, 2 * n2 : 3 * n2, :] = coarse[:, cols]
        last_ref[h] = last[:, cols]


def summaries(queries, keys, values):
    rows, width = queries.shape
    block = pl.BlockSpec((rows, STEP_COLS), lambda i: (0, i))
    return pl.pallas_call(
        summary_kernel,
        grid=(width // STEP_COLS,),
        in_specs=[block, block, block],
        out_specs=[
            pl.BlockSpec((2, rows // 4, STEP_COLS), lambda i: (0, 0, i)),
            pl.BlockSpec((STEP_HEADS, 7 * rows // 16, HD), lambda i: (i, 0, 0)),
            pl.BlockSpec((STEP_HEADS, rows // 16, HD), lambda i: (i, 0, 0)),
        ],
        out_shape=[
            jax.ShapeDtypeStruct((2, rows // 4, width), jnp.bfloat16),
            jax.ShapeDtypeStruct((HEADS, 7 * rows // 16, HD), jnp.bfloat16),
            jax.ShapeDtypeStruct((HEADS, rows // 16, HD), jnp.bfloat16),
        ],
        compiler_params=pltpu.CompilerParams(vmem_limit_bytes=VMEM_LIMIT),
        cost_estimate=pl.CostEstimate(flops=400_000_000, bytes_accessed=5_000_000, transcendentals=0),
        name="summaries",
    )(queries, keys, values)


def place_kernel(heads_ref, sibling_ref, out_ref):
    del heads_ref
    out_ref[...] = sibling_ref[...]


def place_sibling(heads, sibling):
    count, rows, _ = sibling.shape
    place = heads.shape[1] // rows - 1
    return pl.pallas_call(
        place_kernel,
        grid=(1,),
        in_specs=[
            pl.BlockSpec(memory_space=pl.ANY),
            pl.BlockSpec((count, rows, HD), lambda i: (0, 0, 0)),
        ],
        out_specs=pl.BlockSpec((count, rows, HD), lambda i: (0, place, 0)),
        out_shape=jax.ShapeDtypeStruct(heads.shape, heads.dtype),
        input_output_aliases={0: 0},
        compiler_params=pltpu.CompilerParams(vmem_limit_bytes=VMEM_LIMIT),
        name="place_sibling",
    )(heads, sibling)


def with_ones(value):
    return jnp.concatenate([value, jnp.ones_like(value)], 1)


def far_kernel(n2, recv_ref, level_ref, out_ref):
    del level_ref
    blocks = recv_ref.shape[0]
    total = blocks * n2
    keys2 = recv_ref[:, 0:n2, :].reshape(total, HD)
    values2 = recv_ref[:, n2 : 2 * n2, :].reshape(total, HD)
    query2 = recv_ref[:, 2 * n2 : 3 * n2, :].reshape(total, HD)
    last = recv_ref[:, 3 * n2 :, :].reshape(-1, HD)
    rows4 = last.shape[0] // 2
    row = lax.broadcasted_iota(jnp.int32, (rows4, 2 * rows4), 0)
    col = lax.broadcasted_iota(jnp.int32, (rows4, 2 * rows4), 1)
    span = n2 // 4
    spot = row + grid_of((rows4, 2 * rows4), 0, span) * span
    keys4 = dot_bf16(jnp.where(col == spot, 1.0, 0.0).astype(jnp.bfloat16), last)
    values4 = dot_bf16(jnp.where(col == spot + span, 1.0, 0.0).astype(jnp.bfloat16), last)
    group = total // 4
    half = averaging(group // 2, group, 1, 2, 0.5)
    keys3 = [dot_bf16(half, keys2[i * group : (i + 1) * group]) for i in range(4)]
    values3 = [dot_bf16(half, values2[i * group : (i + 1) * group]) for i in range(4)]
    spread2 = averaging(group, group, 2, 2, 0.5)
    spread4 = averaging(group, group, 4, 4, 0.25)
    eye = (
        lax.broadcasted_iota(jnp.int32, (group, group), 0)
        == lax.broadcasted_iota(jnp.int32, (group, group), 1)
    )
    group_blocks = blocks // 4
    pad_lane = grid_of((16, group), 1, n2)
    for g in range(4):
        own = query2[g * group : (g + 1) * group]
        sib = g ^ 1
        far = 2 * ((g // 2) ^ 1)
        key3 = jnp.concatenate(keys3[far : far + 2], 0)
        value3 = jnp.concatenate(values3[far : far + 2], 0)
        scores = [
            dot_nt(own, keys2[sib * group : (sib + 1) * group]) * SCALE + 3.0,
            dot_nt(dot_bf16(spread2, own), key3) * SCALE + 4.0,
            dot_nt(dot_bf16(spread4, own), keys4) * SCALE + 5.0,
        ]
        scores = jnp.concatenate(scores, 1)
        peak = jnp.max(scores, axis=1, keepdims=True)
        weights = jnp.exp2(scores - peak).astype(jnp.bfloat16)
        value = jnp.concatenate([values2[sib * group : (sib + 1) * group], value3, values4], 0)
        both = dot_f32(weights, with_ones(value))
        total_weight = both[:, HD:]
        mean = (both[:, :HD] * pl.reciprocal(total_weight, approx=True)).astype(jnp.bfloat16)
        level = peak + jnp.log2(total_weight)
        level_row = jnp.sum(jnp.where(eye, level, 0.0), axis=0, keepdims=True)
        level_rows = jnp.broadcast_to(level_row, (16, group))
        high = level_rows.astype(jnp.bfloat16).astype(jnp.float32)
        rest = level_rows - high
        mid = rest.astype(jnp.bfloat16).astype(jnp.float32)
        low = rest - mid
        for j in range(group_blocks):
            packed = jnp.zeros_like(high)
            for place, part in enumerate((high, mid, low)):
                turned = pltpu.roll(part, (place - j) * n2 % group, 1)
                packed = jnp.where(pad_lane == place, turned, packed)
            out_ref[g * group_blocks + j, 0:n2, :] = mean[j * n2 : (j + 1) * n2]
            out_ref[g * group_blocks + j, n2 : n2 + 16, :] = packed.astype(jnp.bfloat16)


def far_attention(received, n2, level):
    blocks = received.shape[0]
    vmem = pl.BlockSpec(memory_space=pltpu.VMEM)
    return pl.pallas_call(
        functools.partial(far_kernel, n2),
        in_specs=[vmem, pl.BlockSpec(memory_space=pl.ANY)],
        out_specs=vmem,
        out_shape=jax.ShapeDtypeStruct((blocks, n2 + 16, HD), jnp.bfloat16),
        compiler_params=pltpu.CompilerParams(vmem_limit_bytes=VMEM_LIMIT),
        cost_estimate=pl.CostEstimate(
            flops=200_000_000, bytes_accessed=1_000_000, transcendentals=200_000
        ),
        name="far_attention",
    )(received, level)


def softmax_parts(scores, offsets, top):
    chunks = [[s[:, i : i + HD] for i in range(0, s.shape[1], HD)] for s in scores]
    for parts, offset in zip(chunks, offsets):
        most = functools.reduce(jnp.maximum, parts) * SCALE + offset
        top = most if top is None else jnp.maximum(top, most)
    peak = jnp.broadcast_to(jnp.max(top, axis=1, keepdims=True), top.shape)
    weights = []
    for parts, offset in zip(chunks, offsets):
        shift = peak - offset
        weights += [jnp.exp2(s * SCALE - shift).astype(jnp.bfloat16) for s in parts]
    return weights, peak


def chip_kernel(q_ref, k_ref, v_ref, km_ref, vm_ref, f2_ref, mean_ref, level_ref):
    del f2_ref
    rows = q_ref.shape[0]
    step = pl.program_id(0)
    lane = lax.broadcasted_iota(jnp.int32, (rows, HD), 1)

    def scores_of(h):
        cols = slice(h * HD, (h + 1) * HD)
        return [dot_nt(q_ref[:, cols], ref[:, cols]) for ref in (k_ref, km_ref)]

    levels = jnp.zeros((rows, HD), jnp.float32)
    following = scores_of(0)
    for h in range(STEP_HEADS):
        current = following
        if h + 1 < STEP_HEADS:
            following = scores_of(h + 1)
        cols = slice(h * HD, (h + 1) * HD)
        weights, peak = softmax_parts(current, [0.0, 0.0], None)
        value = jnp.concatenate([v_ref[:, cols], vm_ref[:, cols]], 0)
        both = dot_f32(jnp.concatenate(weights, 1), with_ones(value))
        total = both[:, HD:]
        mean_ref[:, cols] = (both[:, :HD] * pl.reciprocal(total, approx=True)).astype(jnp.bfloat16)
        levels = jnp.where(lane == h, peak + jnp.log2(total), levels)
    level_ref[0] = levels


def chip_attention(q, k, v, k_mate, v_mate, far2):
    rows, width = q.shape
    steps = width // STEP_COLS
    block = pl.BlockSpec((rows, STEP_COLS), lambda i: (0, i))
    return pl.pallas_call(
        chip_kernel,
        grid=(steps,),
        in_specs=[block] * 5 + [pl.BlockSpec(memory_space=pl.ANY)],
        out_specs=[block, pl.BlockSpec((1, rows, HD), lambda i: (i, 0, 0))],
        out_shape=[
            jax.ShapeDtypeStruct((rows, width), jnp.bfloat16),
            jax.ShapeDtypeStruct((steps, rows, HD), jnp.float32),
        ],
        compiler_params=pltpu.CompilerParams(vmem_limit_bytes=VMEM_LIMIT),
        cost_estimate=pl.CostEstimate(
            flops=2_000_000_000, bytes_accessed=7_000_000, transcendentals=2_000_000
        ),
        name="chip_attention",
    )(q, k, v, k_mate, v_mate, far2)


def cross_kernel(
    bias_ref, q_ref, kc_ref, f1_ref, f2_ref, mean_ref, level_ref,
    weight_ref, sum_ref, peak_ref, total_ref,
):
    rows = q_ref.shape[0]
    coarse = dot_bf16(averaging(rows, rows, 4, 4, 0.25), q_ref[...])
    lane = lax.broadcasted_iota(jnp.int32, (rows, HD), 1)
    offsets = [bias_ref[0], 2.0]

    def scores_of(h):
        cols = slice(h * HD, (h + 1) * HD)
        far_key = jnp.concatenate([f1_ref[0, :, cols], f2_ref[0, :, cols]], 0)
        return [dot_nt(q_ref[:, cols], kc_ref[:, cols]), dot_nt(coarse[:, cols], far_key)]

    peaks = jnp.zeros((rows, HD), jnp.float32)
    totals = jnp.zeros((rows, HD), jnp.float32)
    following = scores_of(0)
    for h in range(STEP_HEADS):
        scores = following
        if h + 1 < STEP_HEADS:
            following = scores_of(h + 1)
        cols = slice(h * HD, (h + 1) * HD)
        chip = jnp.broadcast_to(level_ref[0, :, h : h + 1], (rows, HD))
        weights, peak = softmax_parts(scores, offsets, chip)
        weight_ref[h] = jnp.concatenate(weights[:-1], 1)
        value = jnp.concatenate([f1_ref[1, :, cols], f2_ref[1, :, cols]], 0)
        both = dot_f32(weights[-1], with_ones(value))
        chip_weight = jnp.exp2(chip - peak)
        sums = both[:, :HD] + chip_weight * mean_ref[:, cols].astype(jnp.float32)
        sum_ref[:, cols] = sums.astype(jnp.bfloat16)
        peaks = jnp.where(lane == h, peak, peaks)
        totals = jnp.where(lane == h, both[:, HD:] + chip_weight, totals)
    peak_ref[0] = peaks
    total_ref[0] = totals


def cross_attention(bias, q, k_cross, far1, far2, mean, level):
    rows, width = q.shape
    block = pl.BlockSpec((rows, STEP_COLS), lambda i: (0, i))
    far_block = pl.BlockSpec((2, rows // 4, STEP_COLS), lambda i: (0, 0, i))
    levels = pl.BlockSpec((1, rows, HD), lambda i: (i, 0, 0))
    return pl.pallas_call(
        cross_kernel,
        grid=(width // STEP_COLS,),
        in_specs=[pl.BlockSpec(memory_space=pltpu.SMEM)]
        + [block] * 2
        + [far_block] * 2
        + [block, levels],
        out_specs=[pl.BlockSpec((STEP_HEADS, rows, rows), lambda i: (i, 0, 0)), block, levels, levels],
        out_shape=[
            jax.ShapeDtypeStruct((HEADS, rows, rows), jnp.bfloat16),
            jax.ShapeDtypeStruct(mean.shape, mean.dtype),
            jax.ShapeDtypeStruct(level.shape, level.dtype),
            jax.ShapeDtypeStruct(level.shape, level.dtype),
        ],
        compiler_params=pltpu.CompilerParams(vmem_limit_bytes=VMEM_LIMIT),
        cost_estimate=pl.CostEstimate(
            flops=2_000_000_000, bytes_accessed=8_000_000, transcendentals=2_000_000
        ),
        name="cross_attention",
    )(bias, q, k_cross, far1, far2, mean, level)


def final_kernel(weight_ref, sum_ref, peak_ref, total_ref, vc_ref, far_ref, out_ref):
    rows = sum_ref.shape[0]
    n2 = far_ref.shape[1] - 16
    row = grid_of((rows, HD), 0, rows // n2)
    lane = lax.broadcasted_iota(jnp.int32, (rows, HD), 1)
    third = (lane & (n2 - 1)) == row
    pick = jnp.where(third & (lane < 3 * n2), 1.0, 0.0).astype(jnp.bfloat16)
    spread = jnp.where(lane == row, 1.0, 0.0).astype(jnp.bfloat16)[:, :n2]

    def products_of(h):
        cols = slice(h * HD, (h + 1) * HD)
        levels = jnp.concatenate([far_ref[h, n2 : n2 + 16, :]] * (HD // 16), 0)
        return (
            dot_f32(weight_ref[h], with_ones(vc_ref[:, cols])),
            dot_nt(pick, levels),
            dot_f32(spread, far_ref[h, 0:n2, :]),
        )

    following = products_of(0)
    for h in range(STEP_HEADS):
        both, far, far_mean = following
        if h + 1 < STEP_HEADS:
            following = products_of(h + 1)
        cols = slice(h * HD, (h + 1) * HD)
        ahead = far - jnp.broadcast_to(peak_ref[0, :, h : h + 1], (rows, HD))
        near_weight = jnp.exp2(jnp.minimum(-ahead, 0.0))
        far_weight = jnp.exp2(jnp.minimum(ahead, 0.0))
        total = both[:, HD:] + jnp.broadcast_to(total_ref[0, :, h : h + 1], (rows, HD))
        total = near_weight * total + far_weight
        sums = both[:, :HD] + sum_ref[:, cols].astype(jnp.float32)
        sums = near_weight * sums + far_weight * far_mean
        out_ref[:, cols] = (sums * pl.reciprocal(total, approx=True)).astype(jnp.bfloat16)


def final_attention(weights, sums, peak, total, v_cross, far):
    rows, width = sums.shape
    block = pl.BlockSpec((rows, STEP_COLS), lambda i: (0, i))
    levels = pl.BlockSpec((1, rows, HD), lambda i: (i, 0, 0))
    return pl.pallas_call(
        final_kernel,
        grid=(width // STEP_COLS,),
        in_specs=[
            pl.BlockSpec((STEP_HEADS, rows, rows), lambda i: (i, 0, 0)),
            block,
            levels,
            levels,
            block,
            pl.BlockSpec((STEP_HEADS,) + far.shape[1:], lambda i: (i, 0, 0)),
        ],
        out_specs=block,
        out_shape=jax.ShapeDtypeStruct((rows, width), jnp.bfloat16),
        compiler_params=pltpu.CompilerParams(vmem_limit_bytes=VMEM_LIMIT),
        cost_estimate=pl.CostEstimate(
            flops=500_000_000, bytes_accessed=6_000_000, transcendentals=1_000_000
        ),
        name="final_attention",
    )(weights, sums, peak, total, v_cross, far)


def body(queries, keys, values):
    devices = lax.axis_size(AXES)
    inner = lax.axis_size("inner")
    index = lax.axis_index(AXES)
    n2 = queries.shape[0] // 8

    def exchange(value, stride):
        return lax.ppermute(value, AXES, [(i, i ^ stride) for i in range(devices)])

    def cross(value):
        pairs = [(i, i + 1) for i in range(1, devices - 1, 2)]
        return lax.ppermute(value, AXES, pairs + [(j, i) for i, j in pairs])

    k_cross = cross(keys)
    k_mate = exchange(keys, 1)
    v_mate = exchange(values, 1)
    first, heads, last = summaries(queries, keys, values)
    sibling = exchange(last, inner)
    packed = place_sibling(heads, sibling)
    received = lax.all_to_all(packed, "inner", 0, 0, tiled=True)
    far1 = exchange(first, 2)
    v_cross = cross(values)
    far2 = exchange(far1, 1)
    mean, level = chip_attention(queries, keys, values, k_mate, v_mate, far2)
    far = far_attention(received, n2, level)
    far = lax.all_to_all(far, "inner", 0, 0, tiled=True)
    edge = (index == 0) | (index == devices - 1)
    bias = jnp.where(edge, jnp.float32(-1e30), 0.0).reshape(1)
    weights, sums, peak, total = cross_attention(
        bias, queries, k_cross, far1, far2, mean, level
    )
    return final_attention(weights, sums, peak, total, v_cross, far)


def solution(mesh):
    spec = P(AXES, None)
    return jax.shard_map(
        body, mesh=mesh, in_specs=(spec, spec, spec), out_specs=spec, check_vma=False
    )
```

time: 83.7 us -> 70.6 us (0.84)
  waiting for transfers between devices: 25.1 us -> 12.4 us
  Pallas kernels: 20.2 us -> 28.2 us
  starting transfers between devices: 31.5 us -> 26.2 us
  local copies, waits for them, and re-layouts: 5.28 us -> 2.88 us
  other arithmetic: 0.87 us -> 0 us
    all_to_all x1, waiting for transfers between devices: 25.1 us -> 1.56 us  [body(): received = lax.all_to_all(packed, 'inner', 0, 0, tiled=True)]
    pallas_call x3 -> x5, Pallas kernels: 14.6 us -> 23.9 us  [the longest x1 7.35 us: cross_attention(): pl.pallas_call(cross_kernel, grid=(width // STEP_COLS,), in_specs=[pl.Blo...]
    all_to_all x1, waiting for transfers between devices: 0.01 us -> 4.42 us  [body(): far = lax.all_to_all(far, 'inner', 0, 0, tiled=True)]
    ppermute x4 -> x2, starting transfers between devices: 11.1 us -> 6.99 us  [cross(): return lax.ppermute(value, AXES, pairs + [(j, i) for i, j in pairs])]
    ppermute x4 -> x2, waiting for transfers between devices: 0.01 us -> 4.04 us  [cross(): return lax.ppermute(value, AXES, pairs + [(j, i) for i, j in pairs])]
    ppermute x3 -> x5, waiting for transfers between devices: 0.01 us -> 2.33 us  [exchange(): return lax.ppermute(value, AXES, [(i, i ^ stride) for i in range(devices)])]
    slice x2 -> x0, local copies, waits for them, and re-layouts: 1.87 us -> none  [body(): far = far_attention(received[:, :3 * n2], received[:, 3 * n2:])]
    all_to_all x1, starting transfers between devices: 10.6 us -> 8.85 us  [body(): received = lax.all_to_all(packed, 'inner', 0, 0, tiled=True)]
  transfers between devices with their start and end apart: 9 -> 9, of which waited for: 1 -> 4; matrix products, arithmetic and copies ran while one was open for 3% -> 0% of each run, Pallas kernels for 14% -> 27%
where the time goes in v1:
time: 70.6 us; the launch traced here: 69.7 us
  Pallas kernels  28.2 us (40%)
  starting transfers between devices  26.2 us (37%)
  waiting for transfers between devices  12.4 us (18%)
  local copies, waits for them, and re-layouts  2.88 us (4%)
    all_to_all x1, starting transfers between devices, body(): received = lax.all_to_all(packed, 'inner', 0, 0, tiled=True)  8.85 us
    pallas_call x1, Pallas kernels, cross_attention(): pl.pallas_call(cross_kernel, grid=(width // STEP_COLS,), in_specs=[pl.Blo...  7.35 us
    ppermute x2, starting transfers between devices, cross(): return lax.ppermute(value, AXES, pairs + [(j, i) for i, j in pairs])  6.99 us
    pallas_call x1, Pallas kernels, chip_attention(): pl.pallas_call(chip_kernel, grid=(steps,), in_specs=[block] * 5 + [pl.Blo...  6.49 us
    all_to_all x1, starting transfers between devices, body(): far = lax.all_to_all(far, 'inner', 0, 0, tiled=True)  5.44 us
    pallas_call x1, Pallas kernels, final_attention(): pl.pallas_call(final_kernel, grid=(width // STEP_COLS,), in_specs=[pl.Blo...  5.11 us
    ppermute x5, starting transfers between devices, exchange(): return lax.ppermute(value, AXES, [(i, i ^ stride) for i in range(devices)])  4.9 us
    all_to_all x1, waiting for transfers between devices, body(): far = lax.all_to_all(far, 'inner', 0, 0, tiled=True)  4.42 us
  transfers between devices with their start and end apart: 9, of which 4 were waited for; matrix products, arithmetic and copies ran while one was open for 0% of the time, Pallas kernels for 27%

profile of v1, /device:TPU:1, one launch (start us, length us, event | category | flops | bytes accessed | tf_op | source)
XLA Modules:
  0.0 69.7 jit_solution(1305407734519360287)
XLA Ops:
  0.0 0.0 copy-start.2
  0.0 0.0 copy-start.1
  0.0 4.3 %summaries.1 = (bf16[2,64,2048]{2,1,0:T(8,128)(2,1)}, bf16[16,112,128]{2,1,0:T(8,128)(2,1)}, bf16[16,16,128]{2,1,0:T(8,128)(2,1)}) custom-call(bf16[256,2048]{1,0:T(8,128)(2,1)} %q_ref.5, bf16[256,2048]{1,0:T(8,128)(2,1)} %k_ref.3, bf16[256,2048]{1,0:T(8,128)(2,1)} %v_ref.3), custom_call_target="tpu_custom_call" | custom-call | flops 400000000 | bytes 5000000 | tf_op jit(solution)/shard_map/summaries/pallas_call | solution.py:68
  4.3 2.5 %collective-permute-start.1 = (bf16[2,64,2048]{2,1,0:T(8,128)(2,1)}, bf16[2,64,2048]{2,1,0:T(8,128)(2,1)S(1)}, u32[]{:S(2)}, u32[]{:S(2)}) collective-permute-start(bf16[2,64,2048]{2,1,0:T(8,128)(2,1)} %get-tuple-element.14), channel_id=1, source_target_pairs={{0,2},{1,3},{2,0},{3,1},{4,6},{5,7},{6,4},{7,5},{8,10},{9,11},{10,... | collective-permute-start | bytes 1572872 | tf_op jit(solution)/shard_map/ppermute | solution.py:381
  6.7 0.0 copy-done.1
  6.7 1.0 %collective-permute-start.3 = (bf16[256,2048]{1,0:T(8,128)(2,1)S(1)}, bf16[256,2048]{1,0:T(8,128)(2,1)}, u32[]{:S(2)}, u32[]{:S(2)}) collective-permute-start(bf16[256,2048]{1,0:T(8,128)(2,1)S(1)} %copy-done.1), channel_id=1, source_target_pairs={{0,1},{1,0},{2,3},{3,2},{4,5},{5,4},{6,7},{7,6},{8,9},{9,8},{10,11... | collective-permute-start | bytes 3145736 | tf_op jit(solution)/shard_map/ppermute | solution.py:381
  7.7 0.0 copy-done.2
  7.7 0.1 collective-permute-start.4
  7.8 1.3 %collective-permute-start.6 = (bf16[16,16,128]{2,1,0:T(8,128)(2,1)}, bf16[16,16,128]{2,1,0:T(8,128)(2,1)S(1)}, u32[]{:S(2)}, u32[]{:S(2)}) collective-permute-start(bf16[16,16,128]{2,1,0:T(8,128)(2,1)} %get-tuple-element.22), channel_id=1, source_target_pairs={{0,16},{1,17},{2,18},{3,19},{4,20},{5,21},{6,22},{7,23},{8,24},{9,... | collective-permute-start | bytes 196616 | tf_op jit(solution)/shard_map/ppermute | solution.py:381
  9.1 2.3 %collective-permute-done.6.sibling_ref = bf16[16,16,128]{2,1,0:T(8,128)(2,1)S(1)} collective-permute-done((bf16[16,16,128]{2,1,0:T(8,128)(2,1)}, bf16[16,16,128]{2,1,0:T(8,128)(2,1)S(1)}, u32[]{:S(2)}, u32[]{:S(2)}) %collective-permute-start.6) | collective-permute-done | bytes 65568 | tf_op jit(solution)/shard_map/ppermute | solution.py:381
  11.4 0.0 copy-start.4
  11.4 0.6 copy-done.4
  12.0 1.5 %place_sibling.1 = bf16[16,112,128]{2,1,0:T(8,128)(2,1)} custom-call(bf16[16,112,128]{2,1,0:T(8,128)(2,1)} %get-tuple-element.21.heads_ref, bf16[16,16,128]{2,1,0:T(8,128)(2,1)} %copy-done.4), custom_call_target="tpu_custom_call", output_to_operand_aliasing={{}: (0, {})} | custom-call | tf_op jit(solution)/shard_map/place_sibling/pallas_call | solution.py:96
  13.5 8.9 %all-to-all-start = ((bf16[16,112,128]{2,1,0:T(8,128)(2,1)}), bf16[16,112,128]{2,1,0:T(8,128)(2,1)S(1)}, u32[]{:S(2)}, u32[]{:S(2)}) async-start(bf16[16,112,128]{2,1,0:T(8,128)(2,1)} %place_sibling.1), calls=%async_computation | async-start | bytes 917504 | tf_op jit(solution)/shard_map/all_to_all | solution.py:393
  22.4 3.5 %collective-permute-start = (bf16[256,2048]{1,0:T(8,128)(2,1)S(1)}, bf16[256,2048]{1,0:T(8,128)(2,1)}, u32[]{:S(2)}, u32[]{:S(2)}) collective-permute-start(bf16[256,2048]{1,0:T(8,128)(2,1)S(1)} %copy-done.1), channel_id=1, source_target_pairs={{1,2},{3,4},{5,6},{7,8},{9,10},{11,12},{13,14},{15,16},{17,18},{19... | collective-permute-start | bytes 3145736 | tf_op jit(solution)/shard_map/ppermute | solution.py:385
  25.9 0.0 collective-permute-done.1.f1_ref
  25.9 0.0 copy-start.5
  25.9 0.1 collective-permute-start.2
  26.0 3.5 %collective-permute-start.5 = (bf16[256,2048]{1,0:T(8,128)(2,1)S(1)}, bf16[256,2048]{1,0:T(8,128)(2,1)}, u32[]{:S(2)}, u32[]{:S(2)}) collective-permute-start(bf16[256,2048]{1,0:T(8,128)(2,1)S(1)} %copy-done.2), channel_id=1, source_target_pairs={{1,2},{3,4},{5,6},{7,8},{9,10},{11,12},{13,14},{15,16},{17,18},{19... | collective-permute-start | bytes 3145736 | tf_op jit(solution)/shard_map/ppermute | solution.py:385
  29.5 0.0 collective-permute-done.2.f2_ref
  29.5 0.0 copy-start.6
  29.5 0.0 collective-permute-done.3.km_ref
  29.5 0.0 collective-permute-done.4.vm_ref
  29.5 0.8 %copy-done.6 = bf16[2,64,2048]{2,1,0:T(8,128)(2,1)} copy-done((bf16[2,64,2048]{2,1,0:T(8,128)(2,1)}, bf16[2,64,2048]{2,1,0:T(8,128)(2,1)S(1)}, u32[]{:S(2)}) %copy-start.6) | copy-done | bytes 524312
  30.3 6.5 %chip_attention.1 = (bf16[256,2048]{1,0:T(8,128)(2,1)}, f32[4,256,128]{2,1,0:T(8,128)}) custom-call(bf16[256,2048]{1,0:T(8,128)(2,1)} %q_ref.5, bf16[256,2048]{1,0:T(8,128)(2,1)} %k_ref.3, bf16[256,2048]{1,0:T(8,128)(2,1)} %v_ref.3, bf16[256,2048]{1,0:T(8,128)(2,1)} %collective-permute-done.3.km_ref, bf16[256,2048]{1,0:T(8,128)(2,1)} %collective-permute-done.4.vm_ref, ...), custom_call_target="tpu_custom_call" | custom-call | flops 2000000000 | bytes 7000000 | tf_op jit(solution)/shard_map/chip_attention/pallas_call | solution.py:235
  36.8 0.0 copy-done.5
  36.8 1.6 %all-to-all-done.recv_ref = bf16[16,112,128]{2,1,0:T(8,128)(2,1)S(1)} async-done(((bf16[16,112,128]{2,1,0:T(8,128)(2,1)}), bf16[16,112,128]{2,1,0:T(8,128)(2,1)S(1)}, u32[]{:S(2)}, u32[]{:S(2)}) %all-to-all-start) | async-done | bytes 458784 | tf_op jit(solution)/shard_map/all_to_all | solution.py:393
  38.4 0.0 copy-start
  38.4 0.8 %copy-done = bf16[16,112,128]{2,1,0:T(8,128)(2,1)} copy-done((bf16[16,112,128]{2,1,0:T(8,128)(2,1)}, bf16[16,112,128]{2,1,0:T(8,128)(2,1)S(1)}, u32[]{:S(2)}) %copy-start) | copy-done | bytes 458776
  39.1 3.5 %far_attention.1 = bf16[16,48,128]{2,1,0:T(8,128)(2,1)} custom-call(bf16[16,112,128]{2,1,0:T(8,128)(2,1)} %copy-done, f32[4,256,128]{2,1,0:T(8,128)} %get-tuple-element.16.level_ref), custom_call_target="tpu_custom_call" | custom-call | flops 200000000 | bytes 1000000 | tf_op jit(solution)/shard_map/far_attention/pallas_call | solution.py:179
  42.6 5.4 %all-to-all-start.1 = ((bf16[16,48,128]{2,1,0:T(8,128)(2,1)}), bf16[16,48,128]{2,1,0:T(8,128)(2,1)S(1)}, u32[]{:S(2)}, u32[]{:S(2)}) async-start(bf16[16,48,128]{2,1,0:T(8,128)(2,1)} %far_attention.1), calls=%async_computation.1 | async-start | bytes 393216 | tf_op jit(solution)/shard_map/all_to_all | solution.py:399
  48.1 0.0 collective-permute-done.kc_ref
  48.1 7.4 %cross_attention.1 = (bf16[16,256,256]{2,1,0:T(8,128)(2,1)}, bf16[256,2048]{1,0:T(8,128)(2,1)}, f32[4,256,128]{2,1,0:T(8,128)}, f32[4,256,128]{2,1,0:T(8,128)}) custom-call(f32[1]{0:T(128)} %bitcast.bias_ref, bf16[256,2048]{1,0:T(8,128)(2,1)} %q_ref.5, bf16[256,2048]{1,0:T(8,128)(2,1)} %collective-permute-done.kc_ref, bf16[2,64,2048]{2,1,0:T(8,128)(2,1)} %copy-done.5, ...), custom_call_target="tpu_custom_call" | custom-call | flops 2000000000 | bytes 8000000 | tf_op jit(solution)/shard_map/cross_attention/pallas_call | solution.py:293
  55.4 4.0 %collective-permute-done.5.vc_ref = bf16[256,2048]{1,0:T(8,128)(2,1)} collective-permute-done((bf16[256,2048]{1,0:T(8,128)(2,1)S(1)}, bf16[256,2048]{1,0:T(8,128)(2,1)}, u32[]{:S(2)}, u32[]{:S(2)}) %collective-permute-start.5) | collective-permute-done | bytes 1048608 | tf_op jit(solution)/shard_map/ppermute | solution.py:385
  59.4 4.4 %all-to-all-done.1.far_ref = bf16[16,48,128]{2,1,0:T(8,128)(2,1)S(1)} async-done(((bf16[16,48,128]{2,1,0:T(8,128)(2,1)}), bf16[16,48,128]{2,1,0:T(8,128)(2,1)S(1)}, u32[]{:S(2)}, u32[]{:S(2)}) %all-to-all-start.1) | async-done | bytes 196640 | tf_op jit(solution)/shard_map/all_to_all | solution.py:399
  63.9 0.0 copy-start.3
  63.9 0.7 copy-done.3
  64.6 5.1 %final_attention.1 = bf16[256,2048]{1,0:T(8,128)(2,1)} custom-call(bf16[16,256,256]{2,1,0:T(8,128)(2,1)} %get-tuple-element.17.weight_ref, bf16[256,2048]{1,0:T(8,128)(2,1)} %get-tuple-element.18.sum_ref, f32[4,256,128]{2,1,0:T(8,128)} %get-tuple-element.19.peak_ref, f32[4,256,128]{2,1,0:T(8,128)} %get-tuple-element.20.total_ref, ...), custom_call_target="tpu_custom_call" | custom-call | flops 500000000 | bytes 6000000 | tf_op jit(solution)/shard_map/final_attention/pallas_call | solution.py:353
Async XLA Ops:
  0.0 7.7 %copy-start.2 = (bf16[256,2048]{1,0:T(8,128)(2,1)S(1)}, bf16[256,2048]{1,0:T(8,128)(2,1)}, u32[]{:S(2)}) copy-start(bf16[256,2048]{1,0:T(8,128)(2,1)} %v_ref.3) | copy-start | bytes 3145732
  0.0 6.7 %copy-start.1 = (bf16[256,2048]{1,0:T(8,128)(2,1)S(1)}, bf16[256,2048]{1,0:T(8,128)(2,1)}, u32[]{:S(2)}) copy-start(bf16[256,2048]{1,0:T(8,128)(2,1)} %k_ref.3) | copy-start | bytes 3145732
  4.3 21.6 %collective-permute-start.1 = (bf16[2,64,2048]{2,1,0:T(8,128)(2,1)}, bf16[2,64,2048]{2,1,0:T(8,128)(2,1)S(1)}, u32[]{:S(2)}, u32[]{:S(2)}) collective-permute-start(bf16[2,64,2048]{2,1,0:T(8,128)(2,1)} %get-tuple-element.14), channel_id=1, source_target_pairs={{0,2},{1,3},{2,0},{3,1},{4,6},{5,7},{6,4},{7,5},{8,10},{9,11},{10,... | collective-permute-start | bytes 1572872 | tf_op jit(solution)/shard_map/ppermute | solution.py:381
  6.7 22.8 %collective-permute-start.3 = (bf16[256,2048]{1,0:T(8,128)(2,1)S(1)}, bf16[256,2048]{1,0:T(8,128)(2,1)}, u32[]{:S(2)}, u32[]{:S(2)}) collective-permute-start(bf16[256,2048]{1,0:T(8,128)(2,1)S(1)} %copy-done.1), channel_id=1, source_target_pairs={{0,1},{1,0},{2,3},{3,2},{4,5},{5,4},{6,7},{7,6},{8,9},{9,8},{10,11... | collective-permute-start | bytes 3145736 | tf_op jit(solution)/shard_map/ppermute | solution.py:381
  7.7 21.8 %collective-permute-start.4 = (bf16[256,2048]{1,0:T(8,128)(2,1)S(1)}, bf16[256,2048]{1,0:T(8,128)(2,1)}, u32[]{:S(2)}, u32[]{:S(2)}) collective-permute-start(bf16[256,2048]{1,0:T(8,128)(2,1)S(1)} %copy-done.2), channel_id=1, source_target_pairs={{0,1},{1,0},{2,3},{3,2},{4,5},{5,4},{6,7},{7,6},{8,9},{9,8},{10,11... | collective-permute-start | bytes 3145736 | tf_op jit(solution)/shard_map/ppermute | solution.py:381
  7.8 3.6 %collective-permute-start.6 = (bf16[16,16,128]{2,1,0:T(8,128)(2,1)}, bf16[16,16,128]{2,1,0:T(8,128)(2,1)S(1)}, u32[]{:S(2)}, u32[]{:S(2)}) collective-permute-start(bf16[16,16,128]{2,1,0:T(8,128)(2,1)} %get-tuple-element.22), channel_id=1, source_target_pairs={{0,16},{1,17},{2,18},{3,19},{4,20},{5,21},{6,22},{7,23},{8,24},{9,... | collective-permute-start | bytes 196616 | tf_op jit(solution)/shard_map/ppermute | solution.py:381
  11.4 0.6 copy-start.4
  13.5 24.8 %all-to-all-start = ((bf16[16,112,128]{2,1,0:T(8,128)(2,1)}), bf16[16,112,128]{2,1,0:T(8,128)(2,1)S(1)}, u32[]{:S(2)}, u32[]{:S(2)}) async-start(bf16[16,112,128]{2,1,0:T(8,128)(2,1)} %place_sibling.1), calls=%async_computation | async-start | bytes 917504 | tf_op jit(solution)/shard_map/all_to_all | solution.py:393
  22.4 25.7 %collective-permute-start = (bf16[256,2048]{1,0:T(8,128)(2,1)S(1)}, bf16[256,2048]{1,0:T(8,128)(2,1)}, u32[]{:S(2)}, u32[]{:S(2)}) collective-permute-start(bf16[256,2048]{1,0:T(8,128)(2,1)S(1)} %copy-done.1), channel_id=1, source_target_pairs={{1,2},{3,4},{5,6},{7,8},{9,10},{11,12},{13,14},{15,16},{17,18},{19... | collective-permute-start | bytes 3145736 | tf_op jit(solution)/shard_map/ppermute | solution.py:385
  25.9 10.9 %copy-start.5 = (bf16[2,64,2048]{2,1,0:T(8,128)(2,1)}, bf16[2,64,2048]{2,1,0:T(8,128)(2,1)S(1)}, u32[]{:S(2)}) copy-start(bf16[2,64,2048]{2,1,0:T(8,128)(2,1)S(1)} %collective-permute-done.1.f1_ref) | copy-start | bytes 1572868
  25.9 3.6 %collective-permute-start.2 = (bf16[2,64,2048]{2,1,0:T(8,128)(2,1)S(1)}, bf16[2,64,2048]{2,1,0:T(8,128)(2,1)S(1)}, u32[]{:S(2)}, u32[]{:S(2)}) collective-permute-start(bf16[2,64,2048]{2,1,0:T(8,128)(2,1)S(1)} %collective-permute-done.1.f1_ref), channel_id=1, source_target_pairs={{0,1},{1,0},{2,3},{3,2},{4,5},{5,4},{6,7},{7,6},{8,9},{9,8},{10,11... | collective-permute-start | bytes 1572872 | tf_op jit(solution)/shard_map/ppermute | solution.py:381
  26.0 33.4 %collective-permute-start.5 = (bf16[256,2048]{1,0:T(8,128)(2,1)S(1)}, bf16[256,2048]{1,0:T(8,128)(2,1)}, u32[]{:S(2)}, u32[]{:S(2)}) collective-permute-start(bf16[256,2048]{1,0:T(8,128)(2,1)S(1)} %copy-done.2), channel_id=1, source_target_pairs={{1,2},{3,4},{5,6},{7,8},{9,10},{11,12},{13,14},{15,16},{17,18},{19... | collective-permute-start | bytes 3145736 | tf_op jit(solution)/shard_map/ppermute | solution.py:385
  29.5 0.8 %copy-start.6 = (bf16[2,64,2048]{2,1,0:T(8,128)(2,1)}, bf16[2,64,2048]{2,1,0:T(8,128)(2,1)S(1)}, u32[]{:S(2)}) copy-start(bf16[2,64,2048]{2,1,0:T(8,128)(2,1)S(1)} %collective-permute-done.2.f2_ref) | copy-start | bytes 1572868
  38.4 0.8 %copy-start = (bf16[16,112,128]{2,1,0:T(8,128)(2,1)}, bf16[16,112,128]{2,1,0:T(8,128)(2,1)S(1)}, u32[]{:S(2)}) copy-start(bf16[16,112,128]{2,1,0:T(8,128)(2,1)S(1)} %all-to-all-done.recv_ref) | copy-start | bytes 1376260
  42.6 21.3 %all-to-all-start.1 = ((bf16[16,48,128]{2,1,0:T(8,128)(2,1)}), bf16[16,48,128]{2,1,0:T(8,128)(2,1)S(1)}, u32[]{:S(2)}, u32[]{:S(2)}) async-start(bf16[16,48,128]{2,1,0:T(8,128)(2,1)} %far_attention.1), calls=%async_computation.1 | async-start | bytes 393216 | tf_op jit(solution)/shard_map/all_to_all | solution.py:399
  63.9 0.7 copy-start.3

commit v2 on v1

--- a/solution.py
+++ b/solution.py
@@ -181,7 +181,7 @@
         in_specs=[vmem, pl.BlockSpec(memory_space=pl.ANY)],
         out_specs=vmem,
         out_shape=jax.ShapeDtypeStruct((blocks, n2 + 16, HD), jnp.bfloat16),
-        compiler_params=pltpu.CompilerParams(vmem_limit_bytes=VMEM_LIMIT),
+        compiler_params=pltpu.CompilerParams(vmem_limit_bytes=48 * 1024 * 1024),
         cost_estimate=pl.CostEstimate(
             flops=200_000_000, bytes_accessed=1_000_000, transcendentals=200_000
         ),
@@ -312,6 +312,26 @@
     )(bias, q, k_cross, far1, far2, mean, level)
 
 
+def gate_kernel(value_ref, other_ref, out_ref):
+    del value_ref, other_ref, out_ref
+
+
+def gate(value, other):
+    anywhere = pl.BlockSpec(memory_space=pl.ANY)
+    return pl.pallas_call(
+        gate_kernel,
+        in_specs=[anywhere, anywhere],
+        out_specs=anywhere,
+        out_shape=jax.ShapeDtypeStruct(value.shape, value.dtype),
+        input_output_aliases={0: 0},
+        compiler_params=pltpu.CompilerParams(vmem_limit_bytes=VMEM_LIMIT),
+        cost_estimate=pl.CostEstimate(
+            flops=500_000_000, bytes_accessed=6_000_000, transcendentals=100_000
+        ),
+        name="gate",
+    )(value, other)
+
+
 def final_kernel(weight_ref, sum_ref, peak_ref, total_ref, vc_ref, far_ref, out_ref):
     rows = sum_ref.shape[0]
     n2 = far_ref.shape[1] - 16
@@ -363,7 +383,7 @@
         ],
         out_specs=block,
         out_shape=jax.ShapeDtypeStruct((rows, width), jnp.bfloat16),
-        compiler_params=pltpu.CompilerParams(vmem_limit_bytes=VMEM_LIMIT),
+        compiler_params=pltpu.CompilerParams(vmem_limit_bytes=56 * 1024 * 1024),
         cost_estimate=pl.CostEstimate(
             flops=500_000_000, bytes_accessed=6_000_000, transcendentals=1_000_000
         ),
@@ -402,6 +422,7 @@
     weights, sums, peak, total = cross_attention(
         bias, queries, k_cross, far1, far2, mean, level
     )
+    v_cross = gate(v_cross, peak)
     return final_attention(weights, sums, peak, total, v_cross, far)
 
 

time: 70.6 us -> 69.7 us (0.987)
  local copies, waits for them, and re-layouts: 2.88 us -> 4.09 us
  Pallas kernels: 28.2 us -> 27.1 us
    all_to_all x1, waiting for transfers between devices: 1.56 us -> 10.2 us  [body(): received = lax.all_to_all(packed, 'inner', 0, 0, tiled=True)]
    ppermute x2, waiting for transfers between devices: 4.04 us -> 0.01 us  [cross(): return lax.ppermute(value, AXES, pairs + [(j, i) for i, j in pairs])]
    all_to_all x1, waiting for transfers between devices: 4.42 us -> 2 us  [body(): far = lax.all_to_all(far, 'inner', 0, 0, tiled=True)]
    ppermute x5, waiting for transfers between devices: 2.33 us -> 0.01 us  [exchange(): return lax.ppermute(value, AXES, [(i, i ^ stride) for i in range(devices)])]
    unnamed x14, local copies, waits for them, and re-layouts: 2.88 us -> 4.09 us
    pallas_call x1, Pallas kernels: 3.48 us -> 2.44 us  [far_attention(): pl.pallas_call(functools.partial(far_kernel, n2), in_specs=[vmem, pl.Bloc...]
    ppermute x2, starting transfers between devices: 6.99 us -> 6.13 us  [cross(): return lax.ppermute(value, AXES, pairs + [(j, i) for i, j in pairs])]
  transfers between devices with their start and end apart: 9 -> 9, of which waited for: 4 -> 2; matrix products, arithmetic and copies ran while one was open for 0% -> 0% of each run, Pallas kernels for 27% -> 26%
where the time goes in v2:
time: 69.7 us; the launch traced here: 69 us
  Pallas kernels  27.1 us (39%)
  starting transfers between devices  25.5 us (37%)
  waiting for transfers between devices  12.2 us (18%)
  local copies, waits for them, and re-layouts  4.09 us (6%)
    all_to_all x1, waiting for transfers between devices, body(): received = lax.all_to_all(packed, 'inner', 0, 0, tiled=True)  10.2 us
    all_to_all x1, starting transfers between devices, body(): received = lax.all_to_all(packed, 'inner', 0, 0, tiled=True)  8.69 us
    pallas_call x1, Pallas kernels, cross_attention(): pl.pallas_call(cross_kernel, grid=(width // STEP_COLS,), in_specs=[pl.Blo...  7.39 us
    pallas_call x1, Pallas kernels, chip_attention(): pl.pallas_call(chip_kernel, grid=(steps,), in_specs=[block] * 5 + [pl.Blo...  6.49 us
    ppermute x2, starting transfers between devices, cross(): return lax.ppermute(value, AXES, pairs + [(j, i) for i, j in pairs])  6.13 us
    all_to_all x1, starting transfers between devices, body(): far = lax.all_to_all(far, 'inner', 0, 0, tiled=True)  5.78 us
    pallas_call x1, Pallas kernels, final_attention(): pl.pallas_call(final_kernel, grid=(width // STEP_COLS,), in_specs=[pl.Blo...  5.12 us
    ppermute x5, starting transfers between devices, exchange(): return lax.ppermute(value, AXES, [(i, i ^ stride) for i in range(devices)])  4.91 us
  transfers between devices with their start and end apart: 9, of which 2 were waited for; matrix products, arithmetic and copies ran while one was open for 0% of the time, Pallas kernels for 26%

profile of v2, /device:TPU:1, one launch (start us, length us, event | category | flops | bytes accessed | tf_op | source)
XLA Modules:
  0.0 69.0 jit_solution(2512078762827725750)
XLA Ops:
  0.0 0.0 copy-start.2
  0.0 4.2 %summaries.1 = (bf16[2,64,2048]{2,1,0:T(8,128)(2,1)}, bf16[16,112,128]{2,1,0:T(8,128)(2,1)}, bf16[16,16,128]{2,1,0:T(8,128)(2,1)}) custom-call(bf16[256,2048]{1,0:T(8,128)(2,1)} %q_ref.5, bf16[256,2048]{1,0:T(8,128)(2,1)} %k_ref.3, bf16[256,2048]{1,0:T(8,128)(2,1)} %v_ref.3), custom_call_target="tpu_custom_call" | custom-call | flops 400000000 | bytes 5000000 | tf_op jit(solution)/shard_map/summaries/pallas_call | solution.py:68
  4.2 2.5 %collective-permute-start.1 = (bf16[2,64,2048]{2,1,0:T(8,128)(2,1)}, bf16[2,64,2048]{2,1,0:T(8,128)(2,1)S(1)}, u32[]{:S(2)}, u32[]{:S(2)}) collective-permute-start(bf16[2,64,2048]{2,1,0:T(8,128)(2,1)} %get-tuple-element.14), channel_id=1, source_target_pairs={{0,2},{1,3},{2,0},{3,1},{4,6},{5,7},{6,4},{7,5},{8,10},{9,11},{10,... | collective-permute-start | bytes 1572872 | tf_op jit(solution)/shard_map/ppermute | solution.py:401
  6.7 0.0 copy-done.2
  6.7 1.0 %collective-permute-start.3 = (bf16[256,2048]{1,0:T(8,128)(2,1)S(1)}, bf16[256,2048]{1,0:T(8,128)(2,1)}, u32[]{:S(2)}, u32[]{:S(2)}) collective-permute-start(bf16[256,2048]{1,0:T(8,128)(2,1)S(1)} %copy-done.2), channel_id=1, source_target_pairs={{0,1},{1,0},{2,3},{3,2},{4,5},{5,4},{6,7},{7,6},{8,9},{9,8},{10,11... | collective-permute-start | bytes 3145736 | tf_op jit(solution)/shard_map/ppermute | solution.py:401
  7.6 0.0 collective-permute-start.4
  7.6 1.3 %collective-permute-start.6 = (bf16[16,16,128]{2,1,0:T(8,128)(2,1)}, bf16[16,16,128]{2,1,0:T(8,128)(2,1)S(1)}, u32[]{:S(2)}, u32[]{:S(2)}) collective-permute-start(bf16[16,16,128]{2,1,0:T(8,128)(2,1)} %get-tuple-element.22), channel_id=1, source_target_pairs={{0,16},{1,17},{2,18},{3,19},{4,20},{5,21},{6,22},{7,23},{8,24},{9,... | collective-permute-start | bytes 196616 | tf_op jit(solution)/shard_map/ppermute | solution.py:401
  8.9 2.6 %collective-permute-start = (bf16[256,2048]{1,0:T(8,128)(2,1)S(1)}, bf16[256,2048]{1,0:T(8,128)(2,1)}, u32[]{:S(2)}, u32[]{:S(2)}) collective-permute-start(bf16[256,2048]{1,0:T(8,128)(2,1)S(1)} %copy-done.2), channel_id=1, source_target_pairs={{1,2},{3,4},{5,6},{7,8},{9,10},{11,12},{13,14},{15,16},{17,18},{19... | collective-permute-start | bytes 3145736 | tf_op jit(solution)/shard_map/ppermute | solution.py:405
  11.5 0.0 collective-permute-done.6.sibling_ref
  11.5 0.0 copy-start.4
  11.5 0.6 copy-done.4
  12.1 1.5 %place_sibling.1 = bf16[16,112,128]{2,1,0:T(8,128)(2,1)} custom-call(bf16[16,112,128]{2,1,0:T(8,128)(2,1)} %get-tuple-element.21.heads_ref, bf16[16,16,128]{2,1,0:T(8,128)(2,1)} %copy-done.4), custom_call_target="tpu_custom_call", output_to_operand_aliasing={{}: (0, {})} | custom-call | tf_op jit(solution)/shard_map/place_sibling/pallas_call | solution.py:96
  13.6 8.7 %all-to-all-start = ((bf16[16,112,128]{2,1,0:T(8,128)(2,1)}), bf16[16,112,128]{2,1,0:T(8,128)(2,1)S(1)}, u32[]{:S(2)}, u32[]{:S(2)}) async-start(bf16[16,112,128]{2,1,0:T(8,128)(2,1)} %place_sibling.1), calls=%async_computation | async-start | bytes 917504 | tf_op jit(solution)/shard_map/all_to_all | solution.py:413
  22.3 0.0 collective-permute-done.1.f1_ref
  22.3 0.0 copy-start.5
  22.3 0.2 collective-permute-start.2
  22.5 3.6 %collective-permute-start.5 = (bf16[256,2048]{1,0:T(8,128)(2,1)}, bf16[256,2048]{1,0:T(8,128)(2,1)S(1)}, u32[]{:S(2)}, u32[]{:S(2)}) collective-permute-start(bf16[256,2048]{1,0:T(8,128)(2,1)} %v_ref.3), channel_id=1, source_target_pairs={{1,2},{3,4},{5,6},{7,8},{9,10},{11,12},{13,14},{15,16},{17,18},{19... | collective-permute-start | bytes 3145736 | tf_op jit(solution)/shard_map/ppermute | solution.py:405
  26.0 0.0 collective-permute-done.2.f2_ref
  26.1 0.0 copy-start.6
  26.1 0.0 collective-permute-done.3.km_ref
  26.1 0.0 collective-permute-done.4.vm_ref
  26.1 0.8 %copy-done.6 = bf16[2,64,2048]{2,1,0:T(8,128)(2,1)} copy-done((bf16[2,64,2048]{2,1,0:T(8,128)(2,1)}, bf16[2,64,2048]{2,1,0:T(8,128)(2,1)S(1)}, u32[]{:S(2)}) %copy-start.6) | copy-done | bytes 524312
  26.9 6.5 %chip_attention.1 = (bf16[256,2048]{1,0:T(8,128)(2,1)}, f32[4,256,128]{2,1,0:T(8,128)}) custom-call(bf16[256,2048]{1,0:T(8,128)(2,1)} %q_ref.5, bf16[256,2048]{1,0:T(8,128)(2,1)} %k_ref.3, bf16[256,2048]{1,0:T(8,128)(2,1)} %v_ref.3, bf16[256,2048]{1,0:T(8,128)(2,1)} %collective-permute-done.3.km_ref, bf16[256,2048]{1,0:T(8,128)(2,1)} %collective-permute-done.4.vm_ref, ...), custom_call_target="tpu_custom_call" | custom-call | flops 2000000000 | bytes 7000000 | tf_op jit(solution)/shard_map/chip_attention/pallas_call | solution.py:235
  33.3 0.0 copy-done.5
  33.4 10.2 %all-to-all-done.recv_ref = bf16[16,112,128]{2,1,0:T(8,128)(2,1)S(1)} async-done(((bf16[16,112,128]{2,1,0:T(8,128)(2,1)}), bf16[16,112,128]{2,1,0:T(8,128)(2,1)S(1)}, u32[]{:S(2)}, u32[]{:S(2)}) %all-to-all-start) | async-done | bytes 458784 | tf_op jit(solution)/shard_map/all_to_all | solution.py:413
  43.6 0.0 copy-start
  43.6 1.0 %copy-done = f32[4,256,128]{2,1,0:T(8,128)S(1)} copy-done((f32[4,256,128]{2,1,0:T(8,128)S(1)}, f32[4,256,128]{2,1,0:T(8,128)}, u32[]{:S(2)}) %copy-start) | copy-done | bytes 524312
  44.6 2.4 %far_attention.1 = bf16[16,48,128]{2,1,0:T(8,128)(2,1)} custom-call(bf16[16,112,128]{2,1,0:T(8,128)(2,1)S(1)} %all-to-all-done.recv_ref, f32[4,256,128]{2,1,0:T(8,128)S(1)} %copy-done), custom_call_target="tpu_custom_call" | custom-call | flops 200000000 | bytes 1000000 | tf_op jit(solution)/shard_map/far_attention/pallas_call | solution.py:179
  47.0 5.8 %all-to-all-start.1 = ((bf16[16,48,128]{2,1,0:T(8,128)(2,1)}), bf16[16,48,128]{2,1,0:T(8,128)(2,1)S(1)}, u32[]{:S(2)}, u32[]{:S(2)}) async-start(bf16[16,48,128]{2,1,0:T(8,128)(2,1)} %far_attention.1), calls=%async_computation.1 | async-start | bytes 393216 | tf_op jit(solution)/shard_map/all_to_all | solution.py:419
  52.8 0.0 collective-permute-done.kc_ref
  52.8 7.4 %cross_attention.1 = (bf16[16,256,256]{2,1,0:T(8,128)(2,1)}, bf16[256,2048]{1,0:T(8,128)(2,1)}, f32[4,256,128]{2,1,0:T(8,128)}, f32[4,256,128]{2,1,0:T(8,128)}) custom-call(f32[1]{0:T(128)} %bitcast.bias_ref, bf16[256,2048]{1,0:T(8,128)(2,1)} %q_ref.5, bf16[256,2048]{1,0:T(8,128)(2,1)} %collective-permute-done.kc_ref, bf16[2,64,2048]{2,1,0:T(8,128)(2,1)} %copy-done.5, ...), custom_call_target="tpu_custom_call" | custom-call | flops 2000000000 | bytes 8000000 | tf_op jit(solution)/shard_map/cross_attention/pallas_call | solution.py:293
  60.2 0.0 collective-permute-done.5.value_ref
  60.2 0.0 copy-start.1
  60.2 1.0 %copy-done.1 = bf16[256,2048]{1,0:T(8,128)(2,1)} copy-done((bf16[256,2048]{1,0:T(8,128)(2,1)}, bf16[256,2048]{1,0:T(8,128)(2,1)S(1)}, u32[]{:S(2)}) %copy-start.1) | copy-done | bytes 1048600
  61.2 2.0 %all-to-all-done.1.far_ref = bf16[16,48,128]{2,1,0:T(8,128)(2,1)S(1)} async-done(((bf16[16,48,128]{2,1,0:T(8,128)(2,1)}), bf16[16,48,128]{2,1,0:T(8,128)(2,1)S(1)}, u32[]{:S(2)}, u32[]{:S(2)}) %all-to-all-start.1) | async-done | bytes 196640 | tf_op jit(solution)/shard_map/all_to_all | solution.py:419
  63.2 0.0 copy-start.3
  63.2 0.7 copy-done.3
  63.9 5.1 %final_attention.1 = bf16[256,2048]{1,0:T(8,128)(2,1)} custom-call(bf16[16,256,256]{2,1,0:T(8,128)(2,1)} %get-tuple-element.17.weight_ref, bf16[256,2048]{1,0:T(8,128)(2,1)} %get-tuple-element.18.sum_ref, f32[4,256,128]{2,1,0:T(8,128)} %get-tuple-element.19.other_ref.peak_ref, f32[4,256,128]{2,1,0:T(8,128)} %get-tuple-element.20.total_ref, ...), custom_call_target="tpu_custom_call" | custom-call | flops 500000000 | bytes 6000000 | tf_op jit(solution)/shard_map/final_attention/pallas_call | solution.py:373
  (1 shorter events, 0.0 us)
Async XLA Ops:
  0.0 6.7 %copy-start.2 = (bf16[256,2048]{1,0:T(8,128)(2,1)S(1)}, bf16[256,2048]{1,0:T(8,128)(2,1)}, u32[]{:S(2)}) copy-start(bf16[256,2048]{1,0:T(8,128)(2,1)} %k_ref.3) | copy-start | bytes 3145732
  4.2 18.1 %collective-permute-start.1 = (bf16[2,64,2048]{2,1,0:T(8,128)(2,1)}, bf16[2,64,2048]{2,1,0:T(8,128)(2,1)S(1)}, u32[]{:S(2)}, u32[]{:S(2)}) collective-permute-start(bf16[2,64,2048]{2,1,0:T(8,128)(2,1)} %get-tuple-element.14), channel_id=1, source_target_pairs={{0,2},{1,3},{2,0},{3,1},{4,6},{5,7},{6,4},{7,5},{8,10},{9,11},{10,... | collective-permute-start | bytes 1572872 | tf_op jit(solution)/shard_map/ppermute | solution.py:401
  6.7 19.4 %collective-permute-start.3 = (bf16[256,2048]{1,0:T(8,128)(2,1)S(1)}, bf16[256,2048]{1,0:T(8,128)(2,1)}, u32[]{:S(2)}, u32[]{:S(2)}) collective-permute-start(bf16[256,2048]{1,0:T(8,128)(2,1)S(1)} %copy-done.2), channel_id=1, source_target_pairs={{0,1},{1,0},{2,3},{3,2},{4,5},{5,4},{6,7},{7,6},{8,9},{9,8},{10,11... | collective-permute-start | bytes 3145736 | tf_op jit(solution)/shard_map/ppermute | solution.py:401
  7.6 18.5 %collective-permute-start.4 = (bf16[256,2048]{1,0:T(8,128)(2,1)}, bf16[256,2048]{1,0:T(8,128)(2,1)}, u32[]{:S(2)}, u32[]{:S(2)}) collective-permute-start(bf16[256,2048]{1,0:T(8,128)(2,1)} %v_ref.3), channel_id=1, source_target_pairs={{0,1},{1,0},{2,3},{3,2},{4,5},{5,4},{6,7},{7,6},{8,9},{9,8},{10,11... | collective-permute-start | bytes 3145736 | tf_op jit(solution)/shard_map/ppermute | solution.py:401
  7.6 3.9 %collective-permute-start.6 = (bf16[16,16,128]{2,1,0:T(8,128)(2,1)}, bf16[16,16,128]{2,1,0:T(8,128)(2,1)S(1)}, u32[]{:S(2)}, u32[]{:S(2)}) collective-permute-start(bf16[16,16,128]{2,1,0:T(8,128)(2,1)} %get-tuple-element.22), channel_id=1, source_target_pairs={{0,16},{1,17},{2,18},{3,19},{4,20},{5,21},{6,22},{7,23},{8,24},{9,... | collective-permute-start | bytes 196616 | tf_op jit(solution)/shard_map/ppermute | solution.py:401
  8.9 43.9 %collective-permute-start = (bf16[256,2048]{1,0:T(8,128)(2,1)S(1)}, bf16[256,2048]{1,0:T(8,128)(2,1)}, u32[]{:S(2)}, u32[]{:S(2)}) collective-permute-start(bf16[256,2048]{1,0:T(8,128)(2,1)S(1)} %copy-done.2), channel_id=1, source_target_pairs={{1,2},{3,4},{5,6},{7,8},{9,10},{11,12},{13,14},{15,16},{17,18},{19... | collective-permute-start | bytes 3145736 | tf_op jit(solution)/shard_map/ppermute | solution.py:405
  11.5 0.6 copy-start.4
  13.6 30.0 %all-to-all-start = ((bf16[16,112,128]{2,1,0:T(8,128)(2,1)}), bf16[16,112,128]{2,1,0:T(8,128)(2,1)S(1)}, u32[]{:S(2)}, u32[]{:S(2)}) async-start(bf16[16,112,128]{2,1,0:T(8,128)(2,1)} %place_sibling.1), calls=%async_computation | async-start | bytes 917504 | tf_op jit(solution)/shard_map/all_to_all | solution.py:413
  22.3 11.1 %copy-start.5 = (bf16[2,64,2048]{2,1,0:T(8,128)(2,1)}, bf16[2,64,2048]{2,1,0:T(8,128)(2,1)S(1)}, u32[]{:S(2)}) copy-start(bf16[2,64,2048]{2,1,0:T(8,128)(2,1)S(1)} %collective-permute-done.1.f1_ref) | copy-start | bytes 1572868
  22.3 3.8 %collective-permute-start.2 = (bf16[2,64,2048]{2,1,0:T(8,128)(2,1)S(1)}, bf16[2,64,2048]{2,1,0:T(8,128)(2,1)S(1)}, u32[]{:S(2)}, u32[]{:S(2)}) collective-permute-start(bf16[2,64,2048]{2,1,0:T(8,128)(2,1)S(1)} %collective-permute-done.1.f1_ref), channel_id=1, source_target_pairs={{0,1},{1,0},{2,3},{3,2},{4,5},{5,4},{6,7},{7,6},{8,9},{9,8},{10,11... | collective-permute-start | bytes 1572872 | tf_op jit(solution)/shard_map/ppermute | solution.py:401
  22.5 37.8 %collective-permute-start.5 = (bf16[256,2048]{1,0:T(8,128)(2,1)}, bf16[256,2048]{1,0:T(8,128)(2,1)S(1)}, u32[]{:S(2)}, u32[]{:S(2)}) collective-permute-start(bf16[256,2048]{1,0:T(8,128)(2,1)} %v_ref.3), channel_id=1, source_target_pairs={{1,2},{3,4},{5,6},{7,8},{9,10},{11,12},{13,14},{15,16},{17,18},{19... | collective-permute-start | bytes 3145736 | tf_op jit(solution)/shard_map/ppermute | solution.py:405
  26.1 0.8 %copy-start.6 = (bf16[2,64,2048]{2,1,0:T(8,128)(2,1)}, bf16[2,64,2048]{2,1,0:T(8,128)(2,1)S(1)}, u32[]{:S(2)}) copy-start(bf16[2,64,2048]{2,1,0:T(8,128)(2,1)S(1)} %collective-permute-done.2.f2_ref) | copy-start | bytes 1572868
  43.6 1.0 %copy-start = (f32[4,256,128]{2,1,0:T(8,128)S(1)}, f32[4,256,128]{2,1,0:T(8,128)}, u32[]{:S(2)}) copy-start(f32[4,256,128]{2,1,0:T(8,128)} %get-tuple-element.16.level_ref) | copy-start | bytes 1572868
  47.0 16.2 %all-to-all-start.1 = ((bf16[16,48,128]{2,1,0:T(8,128)(2,1)}), bf16[16,48,128]{2,1,0:T(8,128)(2,1)S(1)}, u32[]{:S(2)}, u32[]{:S(2)}) async-start(bf16[16,48,128]{2,1,0:T(8,128)(2,1)} %far_attention.1), calls=%async_computation.1 | async-start | bytes 393216 | tf_op jit(solution)/shard_map/all_to_all | solution.py:419
  60.2 1.0 %copy-start.1 = (bf16[256,2048]{1,0:T(8,128)(2,1)}, bf16[256,2048]{1,0:T(8,128)(2,1)S(1)}, u32[]{:S(2)}) copy-start(bf16[256,2048]{1,0:T(8,128)(2,1)S(1)} %collective-permute-done.5.value_ref) | copy-start | bytes 3145732
  63.2 0.7 copy-start.3
